TPU v7x, 256 devices: a whole 4x4x8 slice. The times are simulated.
256 devices in a mesh: gx: 32 (over z, y), gy: 2 (over core), gz: 4 (over x).
Axes of the slice: x: 4, y: 4, z: 8, core: 2. Of those that a mesh axis runs over, the one named last changes fastest.
Arguments:
- source: float32 [4, 4, 4, 128, 8, 512], P(None, None, None, 'gx', 'gy', 'gz'), may hold values from -6 to 6
- coefficient: float32 [128, 8, 512], P('gx', 'gy', 'gz'), may hold values from 0.2 to 5
- orientation: int32 [6, 128, 8, 512], P(None, 'gx', 'gy', 'gz'), may hold values from 0 to 7
Outputs:
- solution: float32 [4, 4, 4, 128, 8, 512], P(None, None, None, 'gx', 'gy', 'gz')
All inputs are finite; a program needn't handle non-finite values.
Results may differ from a plain program's by a relative error of at most 0.0001.
Values sent between devices are 32-bit elements; how exact they have to be, the bound alone decides.
A program may use at most 128 MiB of HBM per device.

v0:
```python
import math

import jax
import jax.numpy as jnp
import numpy as np
from jax import lax
from jax.experimental import pallas as pl
from jax.experimental.pallas import tpu as pltpu
from jax.sharding import PartitionSpec as P

LOC = 2
TAU = 6.0
SHIFT = 1.0
OMEGA = 0.8
KEEP = 0.2
MESH = pl.DeviceIdType.MESH
F32 = jnp.float32


def lagrange(points, node_points):
    table = np.ones((points.shape[0], 4))
    for column in range(4):
        for other in range(4):
            if other != column:
                table[:, column] *= (points - node_points[other]) / (
                    node_points[column] - node_points[other]
                )
    return table


def jacobi_eigen(matrix):
    current = matrix.copy()
    vectors = np.eye(4)
    for sweep in range(12):
        for first in range(3):
            for second in range(first + 1, 4):
                angle = 0.5 * math.atan2(
                    2.0 * current[first, second], current[second, second] - current[first, first]
                )
                cosine = math.cos(angle)
                sine = math.sin(angle)
                rotation = np.eye(4)
                rotation[first, first] = cosine
                rotation[second, second] = cosine
                rotation[first, second] = sine
                rotation[second, first] = -sine
                current = rotation.T @ current @ rotation
                vectors = vectors @ rotation
    return (np.array([current[index, index] for index in range(4)]), vectors)


def tables():
    node_points = np.array([-1.0, -1.0 / math.sqrt(5.0), 1.0 / math.sqrt(5.0), 1.0])
    weights = np.array([1.0, 5.0, 5.0, 1.0]) / 6.0
    derivative = np.zeros((4, 4))
    for column in range(4):
        for other in range(4):
            if other != column:
                term = np.full(4, 1.0 / (node_points[column] - node_points[other]))
                for third in range(4):
                    if third != column and third != other:
                        term = (
                            term
                            * (node_points - node_points[third])
                            / (node_points[column] - node_points[third])
                        )
                derivative[:, column] += term
    stiffness = derivative.T @ (weights[:, None] * derivative)
    stiffness[0, 0] += TAU
    stiffness[3, 3] += TAU
    scale = weights ** (-0.5)
    eigen_values, eigen_vectors = jacobi_eigen(scale[:, None] * stiffness * scale[None, :])
    modes = scale[:, None] * eigen_vectors
    order = sorted(range(4), key=lambda mode: eigen_values[mode])
    eigen_values, modes = (eigen_values[order], modes[:, order])
    child = lagrange((node_points - 1.0) / 2.0, node_points)
    transfer = modes.T @ (weights[:, None] * (child @ modes))
    return (eigen_values, modes, transfer)


LAM, MODES, TRANSFER = tables()
PAR = (1.0, -1.0, 1.0, -1.0)
SIG = MODES[0]
SQ = [float(value * value) for value in SIG]
INTO = SIG[:, None] * MODES.T
MID = [float(MODES[1, mode] / SIG[mode]) for mode in range(4)]
REST = SIG[:, None] * TRANSFER.T / SIG[None, :]
EXT = SIG[:, None] * TRANSFER / SIG[None, :]


def level_scales(level):
    size_x = 2.0**level
    size_y = 2.0 ** min(level, LOC)
    return (size_y * size_y / size_x, size_x, size_x, size_x * size_y * size_y)


def roll(value, shift, axis):
    size = value.shape[axis]
    shift = shift % size
    if shift == 0:
        return value
    return pltpu.roll(value, shift, axis % value.ndim)


def iota(shape, axis):
    return lax.broadcasted_iota(jnp.int32, shape, axis)


def combine(row, parts):
    total = None
    for factor, part in zip(row, parts):
        term = part * float(factor)
        total = term if total is None else total + term
    return total


def into_modes(s0, s1, s2, s3):
    e0, e1, o0, o1 = (s0 + s3, s1 + s2, s0 - s3, s1 - s2)
    return [
        combine((INTO[mode, 0], INTO[mode, 1]), (e0, e1) if PAR[mode] > 0 else (o0, o1))
        for mode in range(4)
    ]


def from_modes(x0, x1, x2, x3):
    even, odd = (x0 + x2, x1 + x3)
    inner_even = x0 * MID[0] + x2 * MID[2]
    inner_odd = x1 * MID[1] + x3 * MID[3]
    return [even + odd, inner_even + inner_odd, inner_even - inner_odd, even - odd]


def restrict4(first, second):
    plus = [a + b for a, b in zip(first, second)]
    minus = [a - b for a, b in zip(first, second)]
    even = (plus[0], minus[1], plus[2], minus[3])
    odd = (minus[0], plus[1], minus[2], plus[3])
    return [combine(REST[mode], even if PAR[mode] > 0 else odd) for mode in range(4)]


def extend4(parts, sign):
    x0, x1, x2, x3 = parts
    out = []
    for mode in range(4):
        same, other = ((x0, x2), (x1, x3))
        row_same, row_other = ((EXT[mode, 0], EXT[mode, 2]), (EXT[mode, 1], EXT[mode, 3]))
        if PAR[mode] < 0:
            same, other, row_same, row_other = (other, same, row_other, row_same)
        out.append(combine(row_same, same) + sign * combine(row_other, other))
    return out


def extend4_pair(parts):
    x0, x1, x2, x3 = parts
    low, high = ([], [])
    for mode in range(4):
        same, other = ((x0, x2), (x1, x3))
        row_same, row_other = ((EXT[mode, 0], EXT[mode, 2]), (EXT[mode, 1], EXT[mode, 3]))
        if PAR[mode] < 0:
            same, other, row_same, row_other = (other, same, row_other, row_same)
        a, b = (combine(row_same, same), combine(row_other, other))
        low.append(a + b)
        high.append(a - b)
    return low, high


def inverse_tables(g_ref, d_ref, coefficient, level):
    wide_x, wide_y, wide_z, volume = level_scales(level)
    done = {}
    for i in range(4):
        for j in range(4):
            for k in range(4):
                key = (i,) + tuple(sorted((j, k)))
                if wide_x == wide_y:
                    key = tuple(sorted((i, j, k)))
                if key not in done:
                    spectrum = float(wide_x * LAM[i] + wide_y * LAM[j] + wide_z * LAM[k])
                    diagonal = coefficient * spectrum + SHIFT * volume
                    done[key] = (OMEGA / diagonal, diagonal)
                g_ref[i, j, k] = done[key][0]
                d_ref[i, j, k] = done[key][1]


def first_guess(x_ref, b_ref, g_ref):
    for i in range(4):
        for j in range(4):
            x_ref[i, j] = g_ref[i, j] * b_ref[i, j]


def face_pair(x_ref, axis, line):
    if axis == 0:
        parts = [x_ref[mode, line] for mode in range(4)]
    elif axis == 1:
        parts = [x_ref[line, mode] for mode in range(4)]
    else:
        parts = [x_ref[line, :, mode] for mode in range(4)]
    even, odd = (parts[0] + parts[2], parts[1] + parts[3])
    return even + odd, even - odd


def flux(b_ref, f_ref, i, j):
    add = b_ref[i, j] + f_ref[0, i % 2, j] * SQ[i] + f_ref[1, j % 2, i] * SQ[j]
    along_z = [f_ref[2, k % 2, i, j] * SQ[k] for k in range(4)]
    return add + jnp.stack(along_z, axis=0)


def sweep(x_ref, b_ref, g_ref, f_ref):
    for i in range(4):
        for j in range(4):
            x_ref[i, j] = x_ref[i, j] * KEEP + g_ref[i, j] * flux(b_ref, f_ref, i, j)


def residual(r_ref, x_ref, b_ref, d_ref, f_ref):
    for i in range(4):
        for j in range(4):
            r_ref[i, j] = flux(b_ref, f_ref, i, j) - d_ref[i, j] * x_ref[i, j]


class Halo:
    def __init__(self, rows, stride, x, b, g, d, r, t, f, coefficient, wide, orientation, signs):
        self.rows, self.stride = (rows, stride)
        self.x, self.b, self.g, self.d, self.r, self.t, self.f = (x, b, g, d, r, t, f)
        self.coefficient, self.wide = (coefficient, wide)
        self.orientation, self.signs = (orientation, signs)

    def send(self, link):
        rows, stride = (self.rows, self.stride)
        low_rows = iota((4, 8, 128), 1) < 4
        lane = iota((rows, 128), 1)
        firsts, lasts = ([], [])
        for j in range(4):
            low, high = face_pair(self.x, 0, j)
            up, down = (roll(high, 4, 1), roll(low, rows - 4, 1))
            self.t[0, 0, j] = up
            self.t[0, 1, j] = down
            firsts.append((up[:, :8], low[:, :8]))
            lasts.append((high[:, rows - 8 :], down[:, rows - 8 :]))
        for j in range(2):
            link.px[0, j] = jnp.where(low_rows, firsts[j][0], lasts[j + 2][0])
            link.px[1, j] = jnp.where(low_rows, firsts[j][1], lasts[j + 2][1])
        link.start_x()
        packed_high = packed_low = jnp.zeros((rows, 128), F32)
        for i in range(4):
            low, high = face_pair(self.x, 2, i)
            self.t[2, 0, i] = roll(high, stride, 2)
            self.t[2, 1, i] = roll(low, 128 - stride, 2)
            for j in range(4):
                spot = 4 * i + j
                packed_high = jnp.where(lane == spot, roll(high[j], spot + stride, 1), packed_high)
                packed_low = jnp.where(lane == spot, roll(low[j], spot, 1), packed_low)
        link.pz[0] = packed_high
        link.pz[1] = packed_low
        link.start_z()
        for i in range(4):
            low, high = face_pair(self.x, 1, i)
            self.t[1, 0, i] = roll(high, stride, 1)
            self.t[1, 1, i] = roll(low, rows - stride, 1)
            link.py[0, i] = high
            link.py[1, i] = low
        link.start_y()

    def merge(self, axis):
        rows = self.rows
        factor = (TAU * self.wide * self.coefficient[...])[None]
        for line in range(4):
            pair = []
            for side in range(2):
                value = self.t[axis, side, line]
                if self.orientation is not None:
                    face = 2 * axis + side
                    swap = jnp.broadcast_to(self.orientation[face][None], (4, rows, 128)) % 2 == 1
                    value = jnp.where(swap, self.t[axis, side, :, line], value)
                    value = value * self.signs[face, line % 2]
                pair.append(value)
            self.f[axis, 0, line] = factor * (pair[0] + pair[1])
            self.f[axis, 1, line] = factor * (pair[0] - pair[1])

    def receive(self, link):
        rows, stride = (self.rows, self.stride)
        link.wait_y()
        inner = iota((4, rows, 128), 1) % 4
        back = 4 - stride
        for i in range(4):
            self.t[1, 0, i] = jnp.where(inner == 0, roll(link.qy[0, i], rows - back, 1), self.t[1, 0, i])
            self.t[1, 1, i] = jnp.where(inner == back, roll(link.qy[1, i], back, 1), self.t[1, 1, i])
        self.merge(1)
        link.wait_z()
        lane = iota((rows, 128), 1)
        high, low = (link.qz[0], link.qz[1])
        for i in range(4):
            for j in range(4):
                spot = 4 * i + j
                self.t[2, 0, i, j] = jnp.where(lane == 0, roll(high, 128 - spot, 1), self.t[2, 0, i, j])
                self.t[2, 1, i, j] = jnp.where(
                    lane == 128 - stride, roll(low, 128 - stride - spot, 1), self.t[2, 1, i, j]
                )
        self.merge(2)
        link.wait_x()
        low_rows = iota((4, 8, 128), 1) < 4
        for j in range(4):
            high, low = (link.qx[0, j % 2], link.qx[1, j % 2])
            if j < 2:
                low = roll(low, 4, 1)
            else:
                high = roll(high, 4, 1)
            self.t[0, 0, j, :, :8] = jnp.where(low_rows, high, self.t[0, 0, j, :, :8])
            self.t[0, 1, j, :, rows - 8 :] = jnp.where(low_rows, self.t[0, 1, j, :, rows - 8 :], low)
        self.merge(0)

    def smooth(self, link):
        self.send(link)
        self.receive(link)
        sweep(self.x, self.b, self.g, self.f)

    def defect(self, link):
        self.send(link)
        self.receive(link)
        residual(self.r, self.x, self.b, self.d, self.f)


class Link:
    def __init__(self, px, qx, py, qy, pz, qz, send, recv, at):
        self.px, self.qx, self.py, self.qy, self.pz, self.qz = (px, qx, py, qy, pz, qz)
        gx, gy, gz = at

        def copy(src, dst, spot, device):
            return pltpu.make_async_remote_copy(
                src_ref=src,
                dst_ref=dst,
                send_sem=send.at[spot],
                recv_sem=recv.at[spot],
                device_id=device,
                device_id_type=MESH,
            )

        self.x_copies = [
            copy(px.at[0], qx.at[0], 0, {"gx": lax.rem(gx + 1, 32)}),
            copy(px.at[1], qx.at[1], 1, {"gx": lax.rem(gx + 31, 32)}),
        ]
        self.z_copies = [
            copy(pz.at[0], qz.at[0], 2, {"gz": lax.rem(gz + 1, 4)}),
            copy(pz.at[1], qz.at[1], 3, {"gz": lax.rem(gz + 3, 4)}),
        ]
        self.y_copies = [copy(py, qy, 4, {"gy": 1 - gy})]

    def start_x(self):
        for item in self.x_copies:
            item.start()

    def start_y(self):
        for item in self.y_copies:
            item.start()

    def start_z(self):
        for item in self.z_copies:
            item.start()

    def wait_x(self):
        for item in self.x_copies:
            item.wait_recv()

    def wait_y(self):
        for item in self.y_copies:
            item.wait_recv()

    def wait_z(self):
        for item in self.z_copies:
            item.wait_recv()

    def close(self):
        for item in self.x_copies + self.y_copies + self.z_copies:
            item.wait_send()


class Whole:
    def __init__(self, level, count, x, b, g, d, r, f, coefficient):
        self.level, self.count = (level, count)
        self.x, self.b, self.g, self.d, self.r, self.f = (x, b, g, d, r, f)
        self.coefficient = coefficient

    def faces(self):
        wide_x, wide_y, wide_z, _ = level_scales(self.level)
        count = self.count
        coefficient = self.coefficient[...][None]
        ends = iota((4, count, 8, 128), 3) % 64
        for line in range(4):
            low, high = face_pair(self.x, 0, line)
            before, after = (roll(high[:, count - 1 :], 1, 2), roll(low[:, :1], 7, 2))
            if count > 1:
                before = jnp.concatenate([before, high[:, : count - 1]], axis=1)
                after = jnp.concatenate([low[:, 1:], after], axis=1)
            factor = coefficient * (TAU * wide_x)
            self.f[0, 0, line] = factor * (before + after)
            self.f[0, 1, line] = factor * (before - after)
            low, high = face_pair(self.x, 1, line)
            factor = coefficient * (TAU * wide_y)
            self.f[1, 0, line] = factor * roll(high + low, 64, 3)
            self.f[1, 1, line] = factor * roll(high - low, 64, 3)
            low, high = face_pair(self.x, 2, line)
            factor = coefficient * (TAU * wide_z)
            before = jnp.where(ends < 4, roll(high, 69, 3), roll(high, 4, 3))
            after = jnp.where(ends >= 60, roll(low, 59, 3), roll(low, 124, 3))
            self.f[2, 0, line] = factor * (before + after)
            self.f[2, 1, line] = factor * (before - after)

    def tables(self):
        inverse_tables(self.g, self.d, self.coefficient[...], self.level)

    def before(self):
        first_guess(self.x, self.b, self.g)
        self.faces()
        sweep(self.x, self.b, self.g, self.f)

    def down(self, coarse):
        self.faces()
        residual(self.r, self.x, self.b, self.d, self.f)
        for j in range(4):
            for block in range(coarse.count):
                first = [self.r[i, j, :, 2 * block] for i in range(4)]
                second = [self.r[i, j, :, 2 * block + 1] for i in range(4)]
                for i, value in enumerate(restrict4(first, second)):
                    coarse.b[i, j, :, block] = value

    def up(self, coarse):
        for j in range(4):
            for block in range(coarse.count):
                low, high = extend4_pair([coarse.x[i, j, :, block] for i in range(4)])
                for i in range(4):
                    self.x[i, j, :, 2 * block] += low[i]
                    self.x[i, j, :, 2 * block + 1] += high[i]
        for step in range(2):
            self.faces()
            sweep(self.x, self.b, self.g, self.f)


def kernel(
    source,
    coefficient,
    orientation,
    out,
    x0, b0, g0, d0, r0, t0, f0, signs,
    x1, b1, g1, d1, r1, t1, f1, c1, w1, v1,
    x2, b2, g2, d2, r2, f2, c2,
    x3, b3, g3, d3, r3, f3, c3,
    x4, b4, g4, d4, r4, f4, c4,
    px, qx, py0, qy0, pz0, qz0, py1, qy1, pz1, qz1,
    cs, call, cown, cin,
    ms, mall, my, mz,
    face_send, face_recv,
    c_send, c_recv, c_send2, c_recv2,
    m_send, m_recv, m_send2, m_recv2,
):
    gx, gy, gz = (lax.axis_index("gx"), lax.axis_index("gy"), lax.axis_index("gz"))
    slow, fast = (gx // 4, lax.rem(gx, 4))
    slow_at = pl.multiple_of(slow * 16, 16)
    slow_at8 = pl.multiple_of(slow * 8, 8)
    offsets = [(a, b) for a in range(8) for b in range(4) if (a, b) != (0, 0)]

    def along_x(a, b):
        return {"gx": lax.rem(slow + a, 8) * 4 + lax.rem(fast + b, 4)}

    up_z, down_z = (lax.rem(gz + 1, 4), lax.rem(gz + 3, 4))
    around = [
        {"gy": 1 - gy},
        {"gz": up_z},
        {"gy": 1 - gy, "gz": up_z},
        {"gz": down_z},
        {"gy": 1 - gy, "gz": down_z},
    ]

    barrier = pltpu.get_barrier_semaphore()
    for a, b in offsets:
        pl.semaphore_signal(barrier, inc=1, device_id=along_x(a, b), device_id_type=MESH)
    for device in around:
        pl.semaphore_signal(barrier, inc=1, device_id=device, device_id_type=MESH)

    for i in range(4):
        for k, value in enumerate(into_modes(*[source[i, :, k] for k in range(4)])):
            b0[i, :, k] = value
    for i in range(4):
        for j, value in enumerate(into_modes(*[b0[i, j] for j in range(4)])):
            b0[i, j] = value
    for j in range(4):
        for i, value in enumerate(into_modes(*[b0[i, j] for i in range(4)])):
            b0[i, j] = value
    inverse_tables(g0, d0, coefficient[...], 0)
    first_guess(x0, b0, g0)
    for face in range(6):
        code = orientation[face]
        one = jnp.ones((16, 128), F32)
        first = jnp.where(code // 2 % 2 == 1, -one, one)
        second = jnp.where(code // 4 == 1, -one, one)
        signs[face, 0] = jnp.stack([one, second, one, second], axis=0)
        signs[face, 1] = jnp.stack([first, first * second, first, first * second], axis=0)

    row8 = iota((8, 128), 0)
    lane8 = iota((8, 128), 1)
    top, bottom = (coefficient[:8], coefficient[8:])
    value = 0.5 * (
        jnp.where(row8 < 4, top, roll(bottom, 4, 0)) + jnp.where(row8 < 4, roll(top, 4, 0), bottom)
    )
    value = 0.5 * (value + roll(value, 7, 0))
    value = 0.5 * (value + roll(value, 127, 1))
    c1[...] = value
    inverse_tables(g1, d1, value, 1)
    value = 0.5 * (value + roll(value, 4, 0))
    value = 0.5 * (value + roll(value, 6, 0))
    cs[...] = 0.5 * (value + roll(value, 126, 1))

    pl.semaphore_wait(barrier, 36)

    def link(level, step):
        spot = 4 * level + step
        py, qy, pz, qz = (py0, qy0, pz0, qz0) if level == 0 else (py1, qy1, pz1, qz1)
        return Link(
            px.at[spot], qx.at[spot], py.at[step], qy.at[step], pz.at[step], qz.at[step],
            face_send.at[spot], face_recv.at[spot], (gx, gy, gz),
        )

    def copy(src, dst, send, recv, device):
        return pltpu.make_async_remote_copy(
            src_ref=src, dst_ref=dst, send_sem=send, recv_sem=recv, device_id=device, device_id_type=MESH
        )

    fine = Halo(16, 1, x0, b0, g0, d0, r0, t0, f0, coefficient, 1.0, orientation, signs)
    mid = Halo(8, 2, x1, b1, g1, d1, r1, t1, f1, c1, 2.0, None, None)
    links = []

    links.append(link(0, 0))
    fine.send(links[-1])
    c_copies = [
        copy(cs, call.at[fast, pl.ds(slow_at8, 8)], c_send.at[a, b], c_recv.at[a, b], along_x(a, b))
        for a, b in offsets
    ]
    for item in c_copies:
        item.start()
    call[fast, pl.ds(slow_at8, 8), :] = cs[...]
    fine.receive(links[-1])
    sweep(x0, b0, g0, f0)
    links.append(link(0, 1))
    fine.send(links[-1])
    for item in c_copies:
        item.wait_recv()
    for block in range(4):
        cown[block] = call[block, pl.ds(0, 8, stride=8), :]
    c_around = [
        copy(cown, cin.at[spot], c_send2.at[spot], c_recv2.at[spot], device)
        for spot, device in enumerate(around)
    ]
    for item in c_around:
        item.start()
    fine.receive(links[-1])
    residual(r0, x0, b0, d0, f0)
    row4 = iota((4, 8, 128), 1)
    lane4 = iota((4, 8, 128), 2)
    for j in range(4):
        first, second = ([], [])
        for i in range(4):
            top, bottom = (r0[i, j, :, :8], r0[i, j, :, 8:])
            first.append(jnp.where(row4 < 4, top, roll(bottom, 4, 1)))
            second.append(jnp.where(row4 < 4, roll(top, 4, 1), bottom))
        for i, value in enumerate(restrict4(first, second)):
            w1[i, j] = value
    for i in range(4):
        first = [w1[i, j] for j in range(4)]
        for j, value in enumerate(restrict4(first, [roll(item, 7, 1) for item in first])):
            v1[i, j] = value
    for i in range(4):
        first = [v1[i, :, k] for k in range(4)]
        for k, value in enumerate(restrict4(first, [roll(item, 127, 2) for item in first])):
            b1[i, :, k] = value

    first_guess(x1, b1, g1)
    links.append(link(1, 0))
    mid.send(links[-1])
    for item in c_around:
        item.wait_recv()
    for block in range(4):
        mine, other = (cown[block], cin[0, block])
        below, below_other, above, above_other = (cin[spot, block] for spot in range(1, 5))
        phase = lane8 % 4
        near = jnp.where(phase == 0, roll(below, 64, 1), roll(mine, 1, 1))
        near = jnp.where(phase == 2, roll(mine, 66, 1), near)
        near = jnp.where(phase == 3, roll(above, 3, 1), near)
        far = jnp.where(phase == 0, below_other, roll(other, 65, 1))
        far = jnp.where(phase == 2, roll(other, 2, 1), far)
        far = jnp.where(phase == 3, roll(above_other, 67, 1), far)
        c2[block] = jnp.where(lane8 < 64, near, far)
    for block in range(2):
        c3[block] = 0.5 * (c2[2 * block] + c2[2 * block + 1])
    c4[0] = 0.5 * (c3[0] + c3[1])
    level2 = Whole(2, 4, x2, b2, g2, d2, r2, f2, c2)
    level3 = Whole(3, 2, x3, b3, g3, d3, r3, f3, c3)
    level4 = Whole(4, 1, x4, b4, g4, d4, r4, f4, c4)
    level2.tables()
    mid.receive(links[-1])
    sweep(x1, b1, g1, f1)
    links.append(link(1, 1))
    mid.send(links[-1])
    level3.tables()
    level4.tables()
    mid.receive(links[-1])
    residual(r1, x1, b1, d1, f1)
    for j in range(4):
        first = [r1[i, j] for i in range(4)]
        for i, value in enumerate(restrict4(first, [roll(item, 4, 1) for item in first])):
            w1[i, j] = value
    for i in range(4):
        first = [w1[i, j] for j in range(4)]
        for j, value in enumerate(restrict4(first, [roll(item, 6, 1) for item in first])):
            v1[i, j] = value
    packed = []
    for i in range(4):
        first = [v1[i, :, k] for k in range(4)]
        total = None
        for k, value in enumerate(restrict4(first, [roll(item, 126, 2) for item in first])):
            total = value if k == 0 else jnp.where(lane4 % 4 == k, roll(value, k, 2), total)
        packed += [total[j] for j in range(4)]
    for line in range(8):
        low, high = (packed[line], packed[line + 8])
        ms[pl.ds(line, 1), :] = jnp.where(lane8 < 64, low, roll(high, 64, 1))[:1]
        ms[pl.ds(line + 8, 1), :] = jnp.where(lane8 < 64, roll(low, 64, 1), high)[:1]

    m_copies = {
        (a, b): copy(ms, mall.at[fast, pl.ds(slow_at, 16)], m_send.at[a, b], m_recv.at[a, b], along_x(a, b))
        for a, b in offsets
    }
    for item in m_copies.values():
        item.start()
    mall[fast, pl.ds(slow_at, 16), :] = ms[...]
    passed = []
    for a in range(8):
        for b in range(4):
            if (a, b) != (0, 0):
                m_copies[a, b].wait_recv()
        start = lax.rem(slow + 8 - a, 8)
        start16 = pl.multiple_of(start * 16, 16)
        start8 = pl.multiple_of(start * 8, 8)
        upper = pl.multiple_of(start * 16 + 8, 8)
        for spot, device in enumerate(around):
            if spot == 0:
                src, dst = (mall.at[:, pl.ds(start16, 16)], my.at[:, pl.ds(start16, 16)])
            else:
                src = mall.at[:, pl.ds(upper if spot < 3 else start16, 8)]
                dst = mz.at[spot - 1, :, pl.ds(start8, 8)]
            item = copy(src, dst, m_send2.at[spot, a], m_recv2.at[spot, a], device)
            item.start()
            passed.append(item)
    for item in passed:
        item.wait_recv()

    def unpack(block, carry):
        odd, pair = (lane8 % 2 == 1, lane8 % 4 >= 2)
        for line in range(8):
            def rows(ref, start, stride):
                return ref[block, pl.ds(start, 8, stride=stride), :]

            near = [
                rows(mz.at[0], line, 8), rows(mall, line, 16), rows(mall, line + 8, 16), rows(mz.at[2], line, 8)
            ]
            far = [
                rows(mz.at[1], line, 8), rows(my, line, 16), rows(my, line + 8, 16), rows(mz.at[3], line, 8)
            ]
            for half in range(2):
                if half == 0:
                    part = [jnp.where(lane8 < 64, a, roll(b, 64, 1)) for a, b in zip(near, far)]
                else:
                    part = [jnp.where(lane8 < 64, roll(a, 64, 1), b) for a, b in zip(near, far)]
                step = [
                    jnp.where(odd, roll(part[1], 1, 1), part[0]),
                    jnp.where(odd, part[1], roll(part[0], 127, 1)),
                    jnp.where(odd, roll(part[3], 1, 1), part[2]),
                    jnp.where(odd, part[3], roll(part[2], 127, 1)),
                ]
                last = [
                    jnp.where(pair, roll(step[2], 2, 1), step[0]),
                    jnp.where(pair, roll(step[3], 2, 1), step[1]),
                    jnp.where(pair, step[2], roll(step[0], 126, 1)),
                    jnp.where(pair, step[3], roll(step[1], 126, 1)),
                ]
                mode = line + 8 * half
                for k in range(4):
                    b2[mode // 4, mode % 4, k, block] = last[k]
        return carry

    lax.fori_loop(0, 4, unpack, 0)
    level2.before()
    level2.down(level3)
    level3.before()
    level3.down(level4)
    level4.before()
    level3.up(level4)
    level2.up(level3)

    for i in range(4):
        for j in range(4):
            own = jnp.broadcast_to(x2[i, j, :, fast, pl.ds(slow, 1), :], (4, 8, 128))
            own = jnp.where(lane4 < 64, roll(own, 127, 2), roll(own, 62, 2))
            w1[i, j] = jnp.where(lane4 % 4 < 2, own, roll(own, 2, 2))
    one = jnp.ones((4, 8, 128), F32)
    sign = jnp.where(lane4 % 4 < 2, one, -one)
    for i in range(4):
        for k, value in enumerate(extend4([w1[i, :, k] for k in range(4)], sign)):
            w1[i, :, k] = value
    sign = jnp.where(row4 % 4 < 2, one, -one)
    for i in range(4):
        for j, value in enumerate(extend4([w1[i, j] for j in range(4)], sign)):
            w1[i, j] = value
    sign = jnp.where(row4 < 4, one, -one)
    for j in range(4):
        for i, value in enumerate(extend4([w1[i, j] for i in range(4)], sign)):
            x1[i, j] += value
    for step in range(2):
        links.append(link(1, 2 + step))
        mid.smooth(links[-1])

    for i in range(4):
        for j in range(4):
            own = x1[i, j]
            own = jnp.where(row4 % 2 == 0, own, roll(own, 1, 1))
            w1[i, j] = jnp.where(lane4 % 2 == 0, own, roll(own, 1, 2))
    sign = jnp.where(lane4 % 2 == 0, one, -one)
    for i in range(4):
        for k, value in enumerate(extend4([w1[i, :, k] for k in range(4)], sign)):
            w1[i, :, k] = value
    sign = jnp.where(row4 % 2 == 0, one, -one)
    for i in range(4):
        for j, value in enumerate(extend4([w1[i, j] for j in range(4)], sign)):
            w1[i, j] = value
    for j in range(4):
        parts = []
        for i in range(4):
            own = w1[i, j]
            turned = roll(own, 4, 1)
            low, high = (jnp.where(row4 < 4, own, turned), jnp.where(row4 < 4, turned, own))
            parts.append(jnp.concatenate([low, high], axis=1))
        wide_one = jnp.ones((4, 16, 128), F32)
        sign = jnp.where(iota((4, 16, 128), 1) % 8 < 4, wide_one, -wide_one)
        for i, value in enumerate(extend4(parts, sign)):
            x0[i, j] += value
    for step in range(2):
        links.append(link(0, 2 + step))
        fine.smooth(links[-1])

    for i in range(4):
        for k, value in enumerate(from_modes(*[x0[i, :, k] for k in range(4)])):
            out[i, :, k] = value
    for i in range(4):
        for j, value in enumerate(from_modes(*[out[i, j] for j in range(4)])):
            out[i, j] = value
    for j in range(4):
        for i, value in enumerate(from_modes(*[out[i, j] for i in range(4)])):
            out[i, j] = value

    for item in links:
        item.close()
    for item in c_copies + c_around + list(m_copies.values()) + passed:
        item.wait_send()


def scratch():
    def mem(*shape):
        return pltpu.VMEM(shape, F32)

    modes = (4, 4, 4)
    level0 = [mem(*modes, 16, 128)] * 5 + [
        mem(3, 2, 4, 4, 16, 128), mem(3, 2, 4, 4, 16, 128), mem(6, 2, 4, 16, 128)
    ]
    level1 = [mem(*modes, 8, 128)] * 5 + [
        mem(3, 2, 4, 4, 8, 128), mem(3, 2, 4, 4, 8, 128), mem(8, 128), mem(*modes, 8, 128), mem(*modes, 8, 128)
    ]
    whole = []
    for count in (4, 2, 1):
        whole += [mem(*modes, count, 8, 128)] * 5 + [mem(3, 2, 4, 4, count, 8, 128), mem(count, 8, 128)]
    faces = [
        mem(8, 2, 2, 4, 8, 128), mem(8, 2, 2, 4, 8, 128),
        mem(4, 2, 4, 4, 16, 128), mem(4, 2, 4, 4, 16, 128), mem(4, 2, 16, 128), mem(4, 2, 16, 128),
        mem(4, 2, 4, 4, 8, 128), mem(4, 2, 4, 4, 8, 128), mem(4, 2, 8, 128), mem(4, 2, 8, 128),
    ]
    gathered = [
        mem(8, 128), mem(4, 64, 128), mem(4, 8, 128), mem(5, 4, 8, 128),
        mem(16, 128), mem(4, 128, 128), mem(4, 128, 128), mem(4, 4, 64, 128),
    ]
    dma = pltpu.SemaphoreType.DMA
    sems = [dma((8, 5)), dma((8, 5)), dma((8, 4)), dma((8, 4)), dma((5,)), dma((5,)),
            dma((8, 4)), dma((8, 4)), dma((5, 8)), dma((5, 8))]
    return level0 + level1 + whole + faces + gathered + sems


def local(source, coefficient, orientation):
    vmem = pl.BlockSpec(memory_space=pltpu.VMEM)
    out = pl.pallas_call(
        kernel,
        out_shape=jax.ShapeDtypeStruct((4, 4, 4, 16, 128), F32),
        in_specs=[vmem] * 3,
        out_specs=vmem,
        scratch_shapes=scratch(),
        compiler_params=pltpu.CompilerParams(
            collective_id=0, has_side_effects=True, vmem_limit_bytes=44 * 1024 * 1024
        ),
    )(
        source.reshape(4, 4, 4, 16, 128),
        coefficient.reshape(16, 128),
        orientation.reshape(6, 16, 128),
    )
    return out.reshape(4, 4, 4, 4, 4, 128)


def solution(mesh):
    in_specs = (
        P(None, None, None, "gx", "gy", "gz"),
        P("gx", "gy", "gz"),
        P(None, "gx", "gy", "gz"),
    )
    out_specs = P(None, None, None, "gx", "gy", "gz")
    return jax.shard_map(local, mesh=mesh, in_specs=in_specs, out_specs=out_specs, check_vma=False)
```

profile of v0, /device:TPU:1, one launch (start us, length us, event | category | flops | bytes accessed | tf_op | source)
XLA Modules:
  0.0 73.0 jit_solution(7168005571616203672)
XLA Ops:
  0.0 0.0 copy-start
  0.0 1.0 %copy-done = f32[4,4,4,4,4,128]{5,4,3,2,1,0:T(4,128)S(1)} copy-done((f32[4,4,4,4,4,128]{5,4,3,2,1,0:T(4,128)S(1)}, f32[4,4,4,4,4,128]{5,4,3,2,1,0:T(4,128)}, u32[]{:S(2)}) %copy-start) | copy-done | bytes 524312
  1.0 0.0 copy-start.1
  1.0 0.8 %copy-done.1 = s32[6,4,4,128]{3,2,1,0:T(4,128)S(1)} copy-done((s32[6,4,4,128]{3,2,1,0:T(4,128)S(1)}, s32[6,4,4,128]{3,2,1,0:T(4,128)}, u32[]{:S(2)}) %copy-start.1) | copy-done | bytes 49176
  1.8 0.0 copy-start.2
  1.8 0.7 copy-done.2
  2.5 69.6 %shard_map.37 = f32[4,4,4,16,128]{4,3,2,1,0:T(8,128)S(1)} custom-call(f32[4,4,4,16,128]{4,3,2,1,0:T(8,128)S(1)} %bitcast.5, f32[16,128]{1,0:T(8,128)S(1)} %bitcast.7, s32[6,16,128]{2,1,0:T(8,128)S(1)} %bitcast.6), custom_call_target="tpu_custom_call" | custom-call | tf_op jit(solution)/shard_map/pallas_call | solution.py:791
  72.2 0.8 %copy.5 = f32[4,4,4,4,4,128]{5,4,3,2,1,0:T(4,128)} copy(f32[4,4,4,4,4,128]{5,4,3,2,1,0:T(4,128)S(1)} %bitcast.4) | data formatting | bytes 1048576
Async XLA Ops:
  0.0 1.0 %copy-start = (f32[4,4,4,4,4,128]{5,4,3,2,1,0:T(4,128)S(1)}, f32[4,4,4,4,4,128]{5,4,3,2,1,0:T(4,128)}, u32[]{:S(2)}) copy-start(f32[4,4,4,4,4,128]{5,4,3,2,1,0:T(4,128)} %param.3) | copy-start | bytes 1572868
  1.0 0.8 %copy-start.1 = (s32[6,4,4,128]{3,2,1,0:T(4,128)S(1)}, s32[6,4,4,128]{3,2,1,0:T(4,128)}, u32[]{:S(2)}) copy-start(s32[6,4,4,128]{3,2,1,0:T(4,128)} %param.5) | copy-start | bytes 147460
  1.8 0.7 copy-start.2
where the time goes:
time: 73.4 us; the launch traced here: 73 us
  Pallas kernels  69.6 us (95%)
  local copies, waits for them, and re-layouts  3.33 us (5%)
    pallas_call x1, Pallas kernels, local(): pl.pallas_call(kernel, out_shape=jax.ShapeDtypeStruct((4, 4, 4, 16, 128),...  69.6 us
    unnamed x7, local copies, waits for them, and re-layouts  3.33 us

commit v1 on v0

--- a/solution.py
+++ b/solution.py
@@ -149,6 +149,20 @@
     return out
 
 
+def extend4_mirrored(parts, sign):
+    x0, x1, x2, x3 = parts
+    one, two = ([], [])
+    for mode in range(4):
+        same, other = ((x0, x2), (x1, x3))
+        row_same, row_other = ((EXT[mode, 0], EXT[mode, 2]), (EXT[mode, 1], EXT[mode, 3]))
+        if PAR[mode] < 0:
+            same, other, row_same, row_other = (other, same, row_other, row_same)
+        a, b = (combine(row_same, same), sign * combine(row_other, other))
+        one.append(a + b)
+        two.append(a - b)
+    return one, two
+
+
 def extend4_pair(parts):
     x0, x1, x2, x3 = parts
     low, high = ([], [])
@@ -197,10 +211,17 @@
     return even + odd, even - odd
 
 
+def neighbours(f_ref, i, j):
+    along_z = [f_ref[2, k % 2, i, j] * SQ[k] for k in range(4)]
+    return f_ref[1, j % 2, i] * SQ[j] + jnp.stack(along_z, axis=0)
+
+
+def flux_yz(b_ref, f_ref, i, j):
+    return b_ref[i, j] + neighbours(f_ref, i, j)
+
+
 def flux(b_ref, f_ref, i, j):
-    add = b_ref[i, j] + f_ref[0, i % 2, j] * SQ[i] + f_ref[1, j % 2, i] * SQ[j]
-    along_z = [f_ref[2, k % 2, i, j] * SQ[k] for k in range(4)]
-    return add + jnp.stack(along_z, axis=0)
+    return flux_yz(b_ref, f_ref, i, j) + f_ref[0, i % 2, j] * SQ[i]
 
 
 def sweep(x_ref, b_ref, g_ref, f_ref):
@@ -259,6 +280,11 @@
         link.start_y()
 
     def merge(self, axis):
+        for line, even, odd in self.merged(axis):
+            self.f[axis, 0, line] = even
+            self.f[axis, 1, line] = odd
+
+    def merged(self, axis):
         rows = self.rows
         factor = (TAU * self.wide * self.coefficient[...])[None]
         for line in range(4):
@@ -271,10 +297,9 @@
                     value = jnp.where(swap, self.t[axis, side, :, line], value)
                     value = value * self.signs[face, line % 2]
                 pair.append(value)
-            self.f[axis, 0, line] = factor * (pair[0] + pair[1])
-            self.f[axis, 1, line] = factor * (pair[0] - pair[1])
-
-    def receive(self, link):
+            yield line, factor * (pair[0] + pair[1]), factor * (pair[0] - pair[1])
+
+    def land_y(self, link):
         rows, stride = (self.rows, self.stride)
         link.wait_y()
         inner = iota((4, rows, 128), 1) % 4
@@ -282,7 +307,9 @@
         for i in range(4):
             self.t[1, 0, i] = jnp.where(inner == 0, roll(link.qy[0, i], rows - back, 1), self.t[1, 0, i])
             self.t[1, 1, i] = jnp.where(inner == back, roll(link.qy[1, i], back, 1), self.t[1, 1, i])
-        self.merge(1)
+
+    def land_z(self, link):
+        rows, stride = (self.rows, self.stride)
         link.wait_z()
         lane = iota((rows, 128), 1)
         high, low = (link.qz[0], link.qz[1])
@@ -293,7 +320,9 @@
                 self.t[2, 1, i, j] = jnp.where(
                     lane == 128 - stride, roll(low, 128 - stride - spot, 1), self.t[2, 1, i, j]
                 )
-        self.merge(2)
+
+    def land_x(self, link):
+        rows = self.rows
         link.wait_x()
         low_rows = iota((4, 8, 128), 1) < 4
         for j in range(4):
@@ -304,17 +333,56 @@
                 high = roll(high, 4, 1)
             self.t[0, 0, j, :, :8] = jnp.where(low_rows, high, self.t[0, 0, j, :, :8])
             self.t[0, 1, j, :, rows - 8 :] = jnp.where(low_rows, self.t[0, 1, j, :, rows - 8 :], low)
-        self.merge(0)
-
-    def smooth(self, link):
-        self.send(link)
-        self.receive(link)
-        sweep(self.x, self.b, self.g, self.f)
-
-    def defect(self, link):
-        self.send(link)
-        self.receive(link)
-        residual(self.r, self.x, self.b, self.d, self.f)
+
+    def receive(self, link, defect, between=None):
+        self.land_y(link)
+        self.merge(1)
+        self.land_z(link)
+        self.merge(2)
+        for i in range(4):
+            for j in range(4):
+                add = flux_yz(self.b, self.f, i, j)
+                if defect:
+                    self.r[i, j] = add - self.d[i, j] * self.x[i, j]
+                else:
+                    self.x[i, j] = self.x[i, j] * KEEP + self.g[i, j] * add
+        if between is not None:
+            between()
+        self.land_x(link)
+        for j, even, odd in self.merged(0):
+            for i in range(4):
+                add = (even if i % 2 == 0 else odd) * SQ[i]
+                if defect:
+                    self.r[i, j] += add
+                else:
+                    self.x[i, j] += self.g[i, j] * add
+
+    def correct(self, change, halo):
+        rows, stride = (self.rows, self.stride)
+        row, lane = (iota((4, rows, 128), 1), iota((4, rows, 128), 2))
+        low_rows = iota((4, 8, 128), 1) < 4
+        for line in range(4):
+            low, high = face_pair(change, 0, line)
+            up, down = (roll(high, 4, 1), roll(low, rows - 4, 1))
+            beyond = halo[0, line, :, :8]
+            self.t[0, 0, line] = up
+            self.t[0, 1, line] = down
+            self.t[0, 0, line, :, :8] = jnp.where(low_rows, beyond, up[:, :8])
+            self.t[0, 1, line, :, rows - 8 :] = jnp.where(low_rows, down[:, rows - 8 :], beyond)
+            low, high = face_pair(change, 1, line)
+            beyond = halo[1, line]
+            self.t[1, 0, line] = jnp.where(row % 4 == 0, beyond, roll(high, stride, 1))
+            self.t[1, 1, line] = jnp.where(row % 4 == 4 - stride, beyond, roll(low, rows - stride, 1))
+            low, high = face_pair(change, 2, line)
+            beyond = halo[2, line]
+            self.t[2, 0, line] = jnp.where(lane == 0, beyond, roll(high, stride, 2))
+            self.t[2, 1, line] = jnp.where(lane == 128 - stride, beyond, roll(low, 128 - stride, 2))
+        for axis in range(3):
+            self.merge(axis)
+        for i in range(4):
+            for j in range(4):
+                add = neighbours(self.f, i, j) + self.f[0, i % 2, j] * SQ[i]
+                self.x[i, j] += change[i, j] * KEEP + self.g[i, j] * add
 
 
 class Link:
@@ -432,11 +500,53 @@
             sweep(self.x, self.b, self.g, self.f)
 
 
+class Beyond:
+    def __init__(self, e, g, f, h, coefficient):
+        self.e, self.g, self.f, self.h, self.coefficient = (e, g, f, h, coefficient)
+
+    def smooth(self, count, beyond):
+        factor = (TAU * level_scales(1)[0]) * self.coefficient[:count][None]
+        low_rows = iota((4, 8, 128), 1) < 4
+        row, lane = (iota((4, count, 8, 128), 2) % 4, iota((4, count, 8, 128), 3))
+        for line in range(4):
+            low, high = face_pair(self.e, 0, line)
+            ha, hb, hc = (high[:, block] for block in range(3))
+            la, lb, lc = (low[:, block] for block in range(3))
+            far = self.h[line] if beyond else hc
+            ta, sa = (roll(ha, 4, 1), roll(la, 4, 1))
+            before = [jnp.where(low_rows, roll(hb, 4, 1), ta), jnp.where(low_rows, ta, hc), jnp.where(low_rows, hb, far)]
+            after = [jnp.where(low_rows, sa, roll(lb, 4, 1)), jnp.where(low_rows, lc, sa), jnp.where(low_rows, far, lb)]
+            before, after = (jnp.stack(before[:count], axis=1), jnp.stack(after[:count], axis=1))
+            self.f[0, 0, line, :, :count] = factor * (before + after)
+            self.f[0, 1, line, :, :count] = factor * (before - after)
+            low, high = face_pair(self.e, 1, line)
+            low, high = (low[:, :count], high[:, :count])
+            before = jnp.where(row == 0, roll(high, 5, 2), roll(high, 1, 2))
+            after = jnp.where(row == 3, roll(low, 3, 2), roll(low, 7, 2))
+            self.f[1, 0, line, :, :count] = factor * (before + after)
+            self.f[1, 1, line, :, :count] = factor * (before - after)
+            low, high = face_pair(self.e, 2, line)
+            low, high = (low[:, :count], high[:, :count])
+            before = jnp.where(lane == 0, roll(high, 1, 3), jnp.where(lane == 1, roll(high, 3, 3), roll(high, 2, 3)))
+            after = jnp.where(
+                lane == 126, roll(low, 125, 3), jnp.where(lane == 127, roll(low, 127, 3), roll(low, 126, 3))
+            )
+            self.f[2, 0, line, :, :count] = factor * (before + after)
+            self.f[2, 1, line, :, :count] = factor * (before - after)
+        for i in range(4):
+            for j in range(4):
+                along_z = [self.f[2, k % 2, i, j, :count] * SQ[k] for k in range(4)]
+                add = jnp.stack(along_z, axis=0) + self.f[1, j % 2, i, :, :count] * SQ[j]
+                add = add + self.f[0, i % 2, j, :, :count] * SQ[i]
+                self.e[i, j, :, :count] = self.e[i, j, :, :count] * KEEP + self.g[i, j, :, :count] * add
+
+
 def kernel(
-    source,
-    coefficient,
-    orientation,
+    source_in,
+    coefficient_in,
+    orientation_in,
     out,
+    source, coefficient, orientation, input_sem,
     x0, b0, g0, d0, r0, t0, f0, signs,
     x1, b1, g1, d1, r1, t1, f1, c1, w1, v1,
     x2, b2, g2, d2, r2, f2, c2,
@@ -448,7 +558,18 @@
     face_send, face_recv,
     c_send, c_recv, c_send2, c_recv2,
     m_send, m_recv, m_send2, m_recv2,
+    told,
+    e1, ge, fe, he, ce, de, halo1, halo0, wb,
+    near_y, near_z, near_x, near_send, near_recv, spare,
 ):
+    inputs = [
+        pltpu.make_async_copy(src, dst, input_sem.at[spot])
+        for spot, (src, dst) in enumerate(
+            ((coefficient_in, coefficient), (source_in, source), (orientation_in, orientation))
+        )
+    ]
+    for item in inputs:
+        item.start()
     gx, gy, gz = (lax.axis_index("gx"), lax.axis_index("gy"), lax.axis_index("gz"))
     slow, fast = (gx // 4, lax.rem(gx, 4))
     slow_at = pl.multiple_of(slow * 16, 16)
@@ -457,6 +578,9 @@
 
     def along_x(a, b):
         return {"gx": lax.rem(slow + a, 8) * 4 + lax.rem(fast + b, 4)}
+
+    def beside(step):
+        return {"gx": lax.rem(gx + step + 32, 32)}
 
     up_z, down_z = (lax.rem(gz + 1, 4), lax.rem(gz + 3, 4))
     around = [
@@ -468,11 +592,11 @@
     ]
 
     barrier = pltpu.get_barrier_semaphore()
-    for a, b in offsets:
-        pl.semaphore_signal(barrier, inc=1, device_id=along_x(a, b), device_id_type=MESH)
-    for device in around:
+    for device in (beside(1), beside(-1), {"gy": 1 - gy}, {"gz": up_z}, {"gz": down_z}):
         pl.semaphore_signal(barrier, inc=1, device_id=device, device_id_type=MESH)
 
+    for item in inputs:
+        item.wait()
     for i in range(4):
         for k, value in enumerate(into_modes(*[source[i, :, k] for k in range(4)])):
             b0[i, :, k] = value
@@ -506,7 +630,21 @@
     value = 0.5 * (value + roll(value, 6, 0))
     cs[...] = 0.5 * (value + roll(value, 126, 1))
 
-    pl.semaphore_wait(barrier, 36)
+    pl.semaphore_wait(barrier, 5)
+
+    def tell(step):
+        devices = [beside(2**step), beside(-(2**step))]
+        if step == 0:
+            devices.append({"gy": 1 - gy})
+        for device in devices:
+            pl.semaphore_signal(told.at[step], inc=1, device_id=device, device_id_type=MESH)
+
+    def heard(step):
+        pl.semaphore_wait(told.at[step], 3 if step == 0 else 2)
+        if step < 3:
+            tell(step + 1)
+
+    tell(0)
 
     def link(level, step):
         spot = 4 * level + step
@@ -525,19 +663,110 @@
     mid = Halo(8, 2, x1, b1, g1, d1, r1, t1, f1, c1, 2.0, None, None)
     links = []
 
+    near_copies = [copy(c1, near_y, near_send.at[0], near_recv.at[0], {"gy": 1 - gy})]
+    near_copies[0].start()
+    ring = iota((8, 128), 0) % 4
+
+    def near_step(step):
+        if step == 0:
+            near_copies[0].wait_recv()
+            own, other = (c1[...], near_y[...])
+            value = jnp.where(ring < 2, jnp.where(ring == 0, own, roll(own, 7, 0)),
+                              jnp.where(ring == 2, roll(other, 2, 0), roll(other, 1, 0)))
+            spare[0] = value
+            for spot, device in ((1, {"gz": down_z}), (2, {"gz": up_z})):
+                item = copy(spare.at[0], near_z.at[spot - 1], near_send.at[spot], near_recv.at[spot], device)
+                item.start()
+                near_copies.append(item)
+        elif step == 1:
+            near_copies[1].wait_recv()
+            near_copies[2].wait_recv()
+            outer = jnp.where(lane8 < 64, roll(near_z[0], 1, 1), roll(near_z[1], 1, 1))
+            value = jnp.where(lane8 % 2 == 0, spare[0], outer)
+            spare[1] = value
+            ce[0] = value
+            for spot, device in ((3, beside(-1)), (4, beside(1))):
+                item = copy(spare.at[1], near_x.at[spot - 3], near_send.at[spot], near_recv.at[spot], device)
+                item.start()
+                near_copies.append(item)
+        else:
+            near_copies[3].wait_recv()
+            near_copies[4].wait_recv()
+            after, before = (near_x[0], near_x[1])
+            ce[1] = jnp.where(row8 < 4, after, before)
+            ce[2] = jnp.where(row8 < 4, roll(after, 4, 0), roll(before, 4, 0))
+            inverse_tables(ge, de, ce[...], 1)
+
     links.append(link(0, 0))
     fine.send(links[-1])
+    fine.receive(links[-1], False, lambda: (heard(0), near_step(0)))
+    links.append(link(0, 1))
+    fine.send(links[-1])
+    fine.receive(links[-1], True, lambda: (heard(1), near_step(1)))
+    row4 = iota((4, 8, 128), 1)
+    lane4 = iota((4, 8, 128), 2)
+    for j in range(4):
+        first, second = ([], [])
+        for i in range(4):
+            top, bottom = (r0[i, j, :, :8], r0[i, j, :, 8:])
+            first.append(jnp.where(row4 < 4, top, roll(bottom, 4, 1)))
+            second.append(jnp.where(row4 < 4, roll(top, 4, 1), bottom))
+        for i, value in enumerate(restrict4(first, second)):
+            w1[i, j] = value
+    for i in range(4):
+        first = [w1[i, j] for j in range(4)]
+        for j, value in enumerate(restrict4(first, [roll(item, 7, 1) for item in first])):
+            v1[i, j] = value
+    for i in range(4):
+        first = [v1[i, :, k] for k in range(4)]
+        for k, value in enumerate(restrict4(first, [roll(item, 127, 2) for item in first])):
+            b1[i, :, k] = value
+
+    first_guess(x1, b1, g1)
+    links.append(link(1, 0))
+    mid.send(links[-1])
+    mid.receive(links[-1], False, lambda: (heard(2), near_step(2)))
+    links.append(link(1, 1))
+    mid.send(links[-1])
     c_copies = [
         copy(cs, call.at[fast, pl.ds(slow_at8, 8)], c_send.at[a, b], c_recv.at[a, b], along_x(a, b))
         for a, b in offsets
     ]
-    for item in c_copies:
+
+    def send_coefficients():
+        heard(3)
+        for item in c_copies:
+            item.start()
+        call[fast, pl.ds(slow_at8, 8), :] = cs[...]
+
+    mid.receive(links[-1], True, send_coefficients)
+    for j in range(4):
+        first = [r1[i, j] for i in range(4)]
+        for i, value in enumerate(restrict4(first, [roll(item, 4, 1) for item in first])):
+            w1[i, j] = value
+    for i in range(4):
+        first = [w1[i, j] for j in range(4)]
+        for j, value in enumerate(restrict4(first, [roll(item, 6, 1) for item in first])):
+            v1[i, j] = value
+    packed = []
+    for i in range(4):
+        first = [v1[i, :, k] for k in range(4)]
+        total = None
+        for k, value in enumerate(restrict4(first, [roll(item, 126, 2) for item in first])):
+            total = value if k == 0 else jnp.where(lane4 % 4 == k, roll(value, k, 2), total)
+        packed += [total[j] for j in range(4)]
+    for line in range(8):
+        low, high = (packed[line], packed[line + 8])
+        ms[pl.ds(line, 1), :] = jnp.where(lane8 < 64, low, roll(high, 64, 1))[:1]
+        ms[pl.ds(line + 8, 1), :] = jnp.where(lane8 < 64, roll(low, 64, 1), high)[:1]
+
+    m_copies = {
+        (a, b): copy(ms, mall.at[fast, pl.ds(slow_at, 16)], m_send.at[a, b], m_recv.at[a, b], along_x(a, b))
+        for a, b in offsets
+    }
+    for item in m_copies.values():
         item.start()
-    call[fast, pl.ds(slow_at8, 8), :] = cs[...]
-    fine.receive(links[-1])
-    sweep(x0, b0, g0, f0)
-    links.append(link(0, 1))
-    fine.send(links[-1])
+    mall[fast, pl.ds(slow_at, 16), :] = ms[...]
     for item in c_copies:
         item.wait_recv()
     for block in range(4):
@@ -548,30 +777,29 @@
     ]
     for item in c_around:
         item.start()
-    fine.receive(links[-1])
-    residual(r0, x0, b0, d0, f0)
-    row4 = iota((4, 8, 128), 1)
-    lane4 = iota((4, 8, 128), 2)
-    for j in range(4):
-        first, second = ([], [])
-        for i in range(4):
-            top, bottom = (r0[i, j, :, :8], r0[i, j, :, 8:])
-            first.append(jnp.where(row4 < 4, top, roll(bottom, 4, 1)))
-            second.append(jnp.where(row4 < 4, roll(top, 4, 1), bottom))
-        for i, value in enumerate(restrict4(first, second)):
-            w1[i, j] = value
-    for i in range(4):
-        first = [w1[i, j] for j in range(4)]
-        for j, value in enumerate(restrict4(first, [roll(item, 7, 1) for item in first])):
-            v1[i, j] = value
-    for i in range(4):
-        first = [v1[i, :, k] for k in range(4)]
-        for k, value in enumerate(restrict4(first, [roll(item, 127, 2) for item in first])):
-            b1[i, :, k] = value
-
-    first_guess(x1, b1, g1)
-    links.append(link(1, 0))
+    for i in range(4):
+        for j in range(4):
+            x1[i, j] += g1[i, j] * r1[i, j]
+    links.append(link(1, 2))
     mid.send(links[-1])
+    passed = []
+    for a in range(8):
+        for b in range(4):
+            if (a, b) != (0, 0):
+                m_copies[a, b].wait_recv()
+        start = lax.rem(slow + 8 - a, 8)
+        start16 = pl.multiple_of(start * 16, 16)
+        start8 = pl.multiple_of(start * 8, 8)
+        upper = pl.multiple_of(start * 16 + 8, 8)
+        for spot, device in enumerate(around):
+            if spot == 0:
+                src, dst = (mall.at[:, pl.ds(start16, 16)], my.at[:, pl.ds(start16, 16)])
+            else:
+                src = mall.at[:, pl.ds(upper if spot < 3 else start16, 8)]
+                dst = mz.at[spot - 1, :, pl.ds(start8, 8)]
+            item = copy(src, dst, m_send2.at[spot, a], m_recv2.at[spot, a], device)
+            item.start()
+            passed.append(item)
     for item in c_around:
         item.wait_recv()
     for block in range(4):
@@ -591,60 +819,14 @@
     level2 = Whole(2, 4, x2, b2, g2, d2, r2, f2, c2)
     level3 = Whole(3, 2, x3, b3, g3, d3, r3, f3, c3)
     level4 = Whole(4, 1, x4, b4, g4, d4, r4, f4, c4)
-    level2.tables()
-    mid.receive(links[-1])
-    sweep(x1, b1, g1, f1)
-    links.append(link(1, 1))
+    for level in (level2, level3, level4):
+        level.tables()
+    mid.receive(links[-1], False)
+    links.append(link(1, 3))
     mid.send(links[-1])
-    level3.tables()
-    level4.tables()
-    mid.receive(links[-1])
-    residual(r1, x1, b1, d1, f1)
-    for j in range(4):
-        first = [r1[i, j] for i in range(4)]
-        for i, value in enumerate(restrict4(first, [roll(item, 4, 1) for item in first])):
-            w1[i, j] = value
-    for i in range(4):
-        first = [w1[i, j] for j in range(4)]
-        for j, value in enumerate(restrict4(first, [roll(item, 6, 1) for item in first])):
-            v1[i, j] = value
-    packed = []
-    for i in range(4):
-        first = [v1[i, :, k] for k in range(4)]
-        total = None
-        for k, value in enumerate(restrict4(first, [roll(item, 126, 2) for item in first])):
-            total = value if k == 0 else jnp.where(lane4 % 4 == k, roll(value, k, 2), total)
-        packed += [total[j] for j in range(4)]
-    for line in range(8):
-        low, high = (packed[line], packed[line + 8])
-        ms[pl.ds(line, 1), :] = jnp.where(lane8 < 64, low, roll(high, 64, 1))[:1]
-        ms[pl.ds(line + 8, 1), :] = jnp.where(lane8 < 64, roll(low, 64, 1), high)[:1]
-
-    m_copies = {
-        (a, b): copy(ms, mall.at[fast, pl.ds(slow_at, 16)], m_send.at[a, b], m_recv.at[a, b], along_x(a, b))
-        for a, b in offsets
-    }
-    for item in m_copies.values():
-        item.start()
-    mall[fast, pl.ds(slow_at, 16), :] = ms[...]
-    passed = []
-    for a in range(8):
-        for b in range(4):
-            if (a, b) != (0, 0):
-                m_copies[a, b].wait_recv()
-        start = lax.rem(slow + 8 - a, 8)
-        start16 = pl.multiple_of(start * 16, 16)
-        start8 = pl.multiple_of(start * 8, 8)
-        upper = pl.multiple_of(start * 16 + 8, 8)
-        for spot, device in enumerate(around):
-            if spot == 0:
-                src, dst = (mall.at[:, pl.ds(start16, 16)], my.at[:, pl.ds(start16, 16)])
-            else:
-                src = mall.at[:, pl.ds(upper if spot < 3 else start16, 8)]
-                dst = mz.at[spot - 1, :, pl.ds(start8, 8)]
-            item = copy(src, dst, m_send2.at[spot, a], m_recv2.at[spot, a], device)
-            item.start()
-            passed.append(item)
+    for i in range(4):
+        for j in range(4):
+            x0[i, j] += g0[i, j] * r0[i, j]
     for item in passed:
         item.wait_recv()
 
@@ -691,55 +873,119 @@
     level3.up(level4)
     level2.up(level3)
 
-    for i in range(4):
-        for j in range(4):
-            own = jnp.broadcast_to(x2[i, j, :, fast, pl.ds(slow, 1), :], (4, 8, 128))
-            own = jnp.where(lane4 < 64, roll(own, 127, 2), roll(own, 62, 2))
-            w1[i, j] = jnp.where(lane4 % 4 < 2, own, roll(own, 2, 2))
+    def element(step):
+        place = lax.rem(gx + step + 32, 32)
+        return place // 4, lax.rem(place, 4)
+
+    def take(i, j, step):
+        at, block = element(step)
+        return jnp.broadcast_to(x2[i, j, :, block, pl.ds(at, 1), :], (4, 8, 128))
+
+    def spread(value):
+        value = jnp.where(row4 % 4 < 2, value, roll(value, 64, 2))
+        low = jnp.where(lane4 % 2 == 0, roll(value, 127, 2), roll(value, 126, 2))
+        high = jnp.where(lane4 % 2 == 0, roll(value, 62, 2), roll(value, 65, 2))
+        value = jnp.where(lane4 < 64, low, high)
+        return jnp.where(lane4 % 4 < 2, value, roll(value, 2, 2))
+
     one = jnp.ones((4, 8, 128), F32)
-    sign = jnp.where(lane4 % 4 < 2, one, -one)
-    for i in range(4):
-        for k, value in enumerate(extend4([w1[i, :, k] for k in range(4)], sign)):
+    sign_z = jnp.where(lane4 % 4 < 2, one, -one)
+    sign_y = jnp.where(row4 % 2 == 0, one, -one)
+    sign_x = jnp.where(row4 < 4, one, -one)
+    for i in range(4):
+        for j in range(4):
+            w1[i, j] = spread(take(i, j, 0))
+            wb[i, j] = spread(jnp.where(row4 < 4, take(i, j, 1), take(i, j, -1)))
+    for j in range(4):
+        after = [take(i, j, 2) for i in range(4)]
+        before = [take(i, j, -2) for i in range(4)]
+        low = (after[0] + after[2]) + (after[1] + after[3])
+        high = (before[0] + before[2]) - (before[1] + before[3])
+        he[j] = spread(jnp.where(row4 < 4, low, high))
+    for ref in (w1, wb):
+        for i in range(4):
+            for k, value in enumerate(extend4([ref[i, :, k] for k in range(4)], sign_z)):
+                ref[i, :, k] = value
+        for i in range(4):
+            for j, value in enumerate(extend4([ref[i, j] for j in range(4)], sign_y)):
+                ref[i, j] = value
+    for k, value in enumerate(extend4([he[:, k] for k in range(4)], sign_z)):
+        he[:, k] = value
+    for j, value in enumerate(extend4([he[j] for j in range(4)], sign_y)):
+        he[j] = value
+    for j in range(4):
+        for i, value in enumerate(extend4([w1[i, j] for i in range(4)], sign_x)):
+            e1[i, j, :, 0] = value
+        for i, (value, other) in enumerate(zip(*extend4_mirrored([wb[i, j] for i in range(4)], sign_x))):
+            e1[i, j, :, 1] = value
+            e1[i, j, :, 2] = other
+    beyond = Beyond(e1, ge, fe, he, ce)
+    beyond.smooth(3, True)
+    beyond.smooth(2, False)
+
+    mid.land_y(links[-1])
+    mid.land_z(links[-1])
+    mid.land_x(links[-1])
+
+    def own_rows(value):
+        return jnp.where(row4 % 4 == 2, roll(value, 1, 1), value)
+
+    for line in range(4):
+        parts = [e1[i, line, :, 1] for i in range(4)]
+        even, odd = (parts[0] + parts[2], parts[1] + parts[3])
+        value = own_rows(roll(jnp.where(row4 < 4, even + odd, even - odd), 4, 1))
+        halo1[0, line] = value + jnp.where(row4 < 4, t1[0, 0, line], t1[0, 1, line])
+        parts = [e1[line, j, :, 0] for j in range(4)]
+        even, odd = (parts[0] + parts[2], parts[1] + parts[3])
+        value = jnp.where(row4 % 4 == 0, roll(even - odd, 5, 1), even + odd)
+        halo1[1, line] = value + jnp.where(row4 % 4 == 0, t1[1, 0, line], t1[1, 1, line])
+        parts = [e1[line, :, k, 0] for k in range(4)]
+        even, odd = (parts[0] + parts[2], parts[1] + parts[3])
+        value = own_rows(jnp.where(lane4 < 64, roll(even - odd, 1, 2), roll(even + odd, 125, 2)))
+        halo1[2, line] = value + jnp.where(lane4 < 64, t1[2, 0, line], t1[2, 1, line])
+
+    def fill(value):
+        value = jnp.where(row4 % 2 == 0, value, roll(value, 1, 1))
+        return jnp.where(lane4 % 2 == 0, value, roll(value, 1, 2))
+
+    def doubled(value):
+        turned = roll(value, 4, 1)
+        low, high = (jnp.where(row4 < 4, value, turned), jnp.where(row4 < 4, turned, value))
+        return jnp.concatenate([low, high], axis=1)
+
+    for i in range(4):
+        for j in range(4):
+            w1[i, j] = fill(x1[i, j] + own_rows(e1[i, j, :, 0]))
+    for axis in range(3):
+        for line in range(4):
+            halo1[axis, line] = fill(halo1[axis, line])
+    sign_z = jnp.where(lane4 % 2 == 0, one, -one)
+    wide_one = jnp.ones((4, 16, 128), F32)
+    sign_x = jnp.where(iota((4, 16, 128), 1) % 8 < 4, wide_one, -wide_one)
+    for i in range(4):
+        for k, value in enumerate(extend4([w1[i, :, k] for k in range(4)], sign_z)):
             w1[i, :, k] = value
-    sign = jnp.where(row4 % 4 < 2, one, -one)
-    for i in range(4):
-        for j, value in enumerate(extend4([w1[i, j] for j in range(4)], sign)):
-            w1[i, j] = value
-    sign = jnp.where(row4 < 4, one, -one)
-    for j in range(4):
-        for i, value in enumerate(extend4([w1[i, j] for i in range(4)], sign)):
-            x1[i, j] += value
-    for step in range(2):
-        links.append(link(1, 2 + step))
-        mid.smooth(links[-1])
-
-    for i in range(4):
-        for j in range(4):
-            own = x1[i, j]
-            own = jnp.where(row4 % 2 == 0, own, roll(own, 1, 1))
-            w1[i, j] = jnp.where(lane4 % 2 == 0, own, roll(own, 1, 2))
-    sign = jnp.where(lane4 % 2 == 0, one, -one)
-    for i in range(4):
-        for k, value in enumerate(extend4([w1[i, :, k] for k in range(4)], sign)):
-            w1[i, :, k] = value
-    sign = jnp.where(row4 % 2 == 0, one, -one)
-    for i in range(4):
-        for j, value in enumerate(extend4([w1[i, j] for j in range(4)], sign)):
+    for i in range(4):
+        for j, value in enumerate(extend4([w1[i, j] for j in range(4)], sign_y)):
             w1[i, j] = value
     for j in range(4):
-        parts = []
-        for i in range(4):
-            own = w1[i, j]
-            turned = roll(own, 4, 1)
-            low, high = (jnp.where(row4 < 4, own, turned), jnp.where(row4 < 4, turned, own))
-            parts.append(jnp.concatenate([low, high], axis=1))
-        wide_one = jnp.ones((4, 16, 128), F32)
-        sign = jnp.where(iota((4, 16, 128), 1) % 8 < 4, wide_one, -wide_one)
-        for i, value in enumerate(extend4(parts, sign)):
-            x0[i, j] += value
-    for step in range(2):
-        links.append(link(0, 2 + step))
-        fine.smooth(links[-1])
+        for i, value in enumerate(extend4([doubled(w1[i, j]) for i in range(4)], sign_x)):
+            r0[i, j] = value
+    for axis in range(2):
+        for k, value in enumerate(extend4([halo1[axis, :, k] for k in range(4)], sign_z)):
+            halo1[axis, :, k] = value
+    for line, value in enumerate(extend4([halo1[0, line] for line in range(4)], sign_y)):
+        halo0[0, line, :, :8] = value
+    for line, value in enumerate(extend4([doubled(halo1[1, line]) for line in range(4)], sign_x)):
+        halo0[1, line] = value
+    for line, value in enumerate(extend4([halo1[2, :, line] for line in range(4)], sign_y)):
+        halo1[2, :, line] = value
+    for line, value in enumerate(extend4([doubled(halo1[2, line]) for line in range(4)], sign_x)):
+        halo0[2, line] = value
+    fine.correct(r0, halo0)
+    links.append(link(0, 2))
+    fine.send(links[-1])
+    fine.receive(links[-1], False)
 
     for i in range(4):
         for k, value in enumerate(from_modes(*[x0[i, :, k] for k in range(4)])):
@@ -753,7 +999,7 @@
 
     for item in links:
         item.close()
-    for item in c_copies + c_around + list(m_copies.values()) + passed:
+    for item in near_copies + c_copies + c_around + list(m_copies.values()) + passed:
         item.wait_send()
 
 
@@ -762,6 +1008,8 @@
         return pltpu.VMEM(shape, F32)
 
     modes = (4, 4, 4)
+    dma = pltpu.SemaphoreType.DMA
+    inputs = [mem(*modes, 16, 128), mem(16, 128), pltpu.VMEM((6, 16, 128), jnp.int32), dma((3,))]
     level0 = [mem(*modes, 16, 128)] * 5 + [
         mem(3, 2, 4, 4, 16, 128), mem(3, 2, 4, 4, 16, 128), mem(6, 2, 4, 16, 128)
     ]
@@ -780,10 +1028,15 @@
         mem(8, 128), mem(4, 64, 128), mem(4, 8, 128), mem(5, 4, 8, 128),
         mem(16, 128), mem(4, 128, 128), mem(4, 128, 128), mem(4, 4, 64, 128),
     ]
-    dma = pltpu.SemaphoreType.DMA
     sems = [dma((8, 5)), dma((8, 5)), dma((8, 4)), dma((8, 4)), dma((5,)), dma((5,)),
-            dma((8, 4)), dma((8, 4)), dma((5, 8)), dma((5, 8))]
-    return level0 + level1 + whole + faces + gathered + sems
+            dma((8, 4)), dma((8, 4)), dma((5, 8)), dma((5, 8)),
+            pltpu.SemaphoreType.REGULAR((4,))]
+    extended = [
+        mem(*modes, 3, 8, 128), mem(*modes, 3, 8, 128), mem(3, 2, 4, 4, 3, 8, 128), mem(4, 4, 8, 128),
+        mem(3, 8, 128), mem(*modes, 3, 8, 128), mem(3, 4, 4, 8, 128), mem(3, 4, 4, 16, 128), mem(*modes, 8, 128),
+        mem(8, 128), mem(2, 8, 128), mem(2, 8, 128), dma((5,)), dma((5,)), mem(2, 8, 128),
+    ]
+    return inputs + level0 + level1 + whole + faces + gathered + sems + extended
 
 
 def local(source, coefficient, orientation):
@@ -791,7 +1044,7 @@
     out = pl.pallas_call(
         kernel,
         out_shape=jax.ShapeDtypeStruct((4, 4, 4, 16, 128), F32),
-        in_specs=[vmem] * 3,
+        in_specs=[pl.BlockSpec(memory_space=pl.ANY)] * 3,
         out_specs=vmem,
         scratch_shapes=scratch(),
         compiler_params=pltpu.CompilerParams(

time: 73.4 us -> 66.4 us (0.905)
  Pallas kernels: 69.6 us -> 62.9 us
    pallas_call x1, Pallas kernels: 69.6 us -> 62.9 us  [local(): pl.pallas_call(kernel, out_shape=jax.ShapeDtypeStruct((4, 4, 4, 16, 128),...]
where the time goes in v1:
time: 66.4 us; the launch traced here: 66.2 us
  Pallas kernels  62.9 us (95%)
  local copies, waits for them, and re-layouts  3.33 us (5%)
    pallas_call x1, Pallas kernels, local(): pl.pallas_call(kernel, out_shape=jax.ShapeDtypeStruct((4, 4, 4, 16, 128),...  62.9 us
    unnamed x7, local copies, waits for them, and re-layouts  3.33 us

profile of v1, /device:TPU:1, one launch (start us, length us, event | category | flops | bytes accessed | tf_op | source)
XLA Modules:
  0.0 66.2 jit_solution(5864115836548349342)
XLA Ops:
  0.0 0.0 copy-start
  0.0 1.0 %copy-done = f32[4,4,4,4,4,128]{5,4,3,2,1,0:T(4,128)S(1)} copy-done((f32[4,4,4,4,4,128]{5,4,3,2,1,0:T(4,128)S(1)}, f32[4,4,4,4,4,128]{5,4,3,2,1,0:T(4,128)}, u32[]{:S(2)}) %copy-start) | copy-done | bytes 524312
  1.0 0.0 copy-start.1
  1.0 0.8 %copy-done.1 = s32[6,4,4,128]{3,2,1,0:T(4,128)S(1)} copy-done((s32[6,4,4,128]{3,2,1,0:T(4,128)S(1)}, s32[6,4,4,128]{3,2,1,0:T(4,128)}, u32[]{:S(2)}) %copy-start.1) | copy-done | bytes 49176
  1.8 0.0 copy-start.2
  1.8 0.7 %copy-done.2 = f32[4,4,128]{2,1,0:T(4,128)S(1)} copy-done((f32[4,4,128]{2,1,0:T(4,128)S(1)}, f32[4,4,128]{2,1,0:T(4,128)}, u32[]{:S(2)}) %copy-start.2) | copy-done | bytes 8216
  2.5 62.9 %shard_map.37 = f32[4,4,4,16,128]{4,3,2,1,0:T(8,128)S(1)} custom-call(f32[4,4,4,16,128]{4,3,2,1,0:T(8,128)S(1)} %bitcast.5, f32[16,128]{1,0:T(8,128)S(1)} %bitcast.7, s32[6,16,128]{2,1,0:T(8,128)S(1)} %bitcast.6), custom_call_target="tpu_custom_call" | custom-call | tf_op jit(solution)/shard_map/pallas_call | solution.py:1044
  65.4 0.8 %copy.5 = f32[4,4,4,4,4,128]{5,4,3,2,1,0:T(4,128)} copy(f32[4,4,4,4,4,128]{5,4,3,2,1,0:T(4,128)S(1)} %bitcast.4) | data formatting | bytes 1048576
Async XLA Ops:
  0.0 1.0 %copy-start = (f32[4,4,4,4,4,128]{5,4,3,2,1,0:T(4,128)S(1)}, f32[4,4,4,4,4,128]{5,4,3,2,1,0:T(4,128)}, u32[]{:S(2)}) copy-start(f32[4,4,4,4,4,128]{5,4,3,2,1,0:T(4,128)} %param.3) | copy-start | bytes 1572868
  1.0 0.8 %copy-start.1 = (s32[6,4,4,128]{3,2,1,0:T(4,128)S(1)}, s32[6,4,4,128]{3,2,1,0:T(4,128)}, u32[]{:S(2)}) copy-start(s32[6,4,4,128]{3,2,1,0:T(4,128)} %param.5) | copy-start | bytes 147460
  1.8 0.7 %copy-start.2 = (f32[4,4,128]{2,1,0:T(4,128)S(1)}, f32[4,4,128]{2,1,0:T(4,128)}, u32[]{:S(2)}) copy-start(f32[4,4,128]{2,1,0:T(4,128)} %param.4) | copy-start | bytes 24580

commit v2 on v1

--- a/solution.py
+++ b/solution.py
@@ -82,6 +82,7 @@
 PAR = (1.0, -1.0, 1.0, -1.0)
 SIG = MODES[0]
 SQ = [float(value * value) for value in SIG]
+RATIO = [1.0, 1.0, SQ[2] / SQ[0], SQ[3] / SQ[1]]
 INTO = SIG[:, None] * MODES.T
 MID = [float(MODES[1, mode] / SIG[mode]) for mode in range(4)]
 REST = SIG[:, None] * TRANSFER.T / SIG[None, :]
@@ -211,29 +212,49 @@
     return even + odd, even - odd
 
 
+def weigh(value, mode):
+    return value if mode < 2 else value * RATIO[mode]
+
+
 def neighbours(f_ref, i, j):
-    along_z = [f_ref[2, k % 2, i, j] * SQ[k] for k in range(4)]
-    return f_ref[1, j % 2, i] * SQ[j] + jnp.stack(along_z, axis=0)
+    along_z = [weigh(f_ref[2, k % 2, i, j], k) for k in range(4)]
+    return weigh(f_ref[1, j % 2, i], j) + jnp.stack(along_z, axis=0)
 
 
 def flux_yz(b_ref, f_ref, i, j):
     return b_ref[i, j] + neighbours(f_ref, i, j)
 
 
-def flux(b_ref, f_ref, i, j):
-    return flux_yz(b_ref, f_ref, i, j) + f_ref[0, i % 2, j] * SQ[i]
+def face_pair2(x_ref, axis, first, second):
+    if axis == 0:
+        parts = [x_ref[mode, first, second] for mode in range(4)]
+    elif axis == 1:
+        parts = [x_ref[first, mode, second] for mode in range(4)]
+    else:
+        parts = [x_ref[first, second, mode] for mode in range(4)]
+    even, odd = (parts[0] + parts[2], parts[1] + parts[3])
+    return even + odd, even - odd
+
+
+def flux_at(f_ref, i, j, k):
+    add = weigh(f_ref[0, i % 2, j, k], i) + weigh(f_ref[1, j % 2, i, k], j)
+    return add + weigh(f_ref[2, k % 2, i, j], k)
 
 
 def sweep(x_ref, b_ref, g_ref, f_ref):
     for i in range(4):
         for j in range(4):
-            x_ref[i, j] = x_ref[i, j] * KEEP + g_ref[i, j] * flux(b_ref, f_ref, i, j)
+            for k in range(4):
+                add = b_ref[i, j, k] + flux_at(f_ref, i, j, k)
+                x_ref[i, j, k] = x_ref[i, j, k] * KEEP + g_ref[i, j, k] * add
 
 
 def residual(r_ref, x_ref, b_ref, d_ref, f_ref):
     for i in range(4):
         for j in range(4):
-            r_ref[i, j] = flux(b_ref, f_ref, i, j) - d_ref[i, j] * x_ref[i, j]
+            for k in range(4):
+                add = b_ref[i, j, k] + flux_at(f_ref, i, j, k)
+                r_ref[i, j, k] = add - d_ref[i, j, k] * x_ref[i, j, k]
 
 
 class Halo:
@@ -286,7 +307,9 @@
 
     def merged(self, axis):
         rows = self.rows
-        factor = (TAU * self.wide * self.coefficient[...])[None]
+        value = self.coefficient[...]
+        even = (value * (TAU * self.wide * SQ[0]))[None]
+        odd = (value * (TAU * self.wide * SQ[1]))[None]
         for line in range(4):
             pair = []
             for side in range(2):
@@ -297,7 +320,7 @@
                     value = jnp.where(swap, self.t[axis, side, :, line], value)
                     value = value * self.signs[face, line % 2]
                 pair.append(value)
-            yield line, factor * (pair[0] + pair[1]), factor * (pair[0] - pair[1])
+            yield line, even * (pair[0] + pair[1]), odd * (pair[0] - pair[1])
 
     def land_y(self, link):
         rows, stride = (self.rows, self.stride)
@@ -351,7 +374,7 @@
         self.land_x(link)
         for j, even, odd in self.merged(0):
             for i in range(4):
-                add = (even if i % 2 == 0 else odd) * SQ[i]
+                add = weigh(even if i % 2 == 0 else odd, i)
                 if defect:
                     self.r[i, j] += add
                 else:
@@ -381,7 +404,7 @@
             self.merge(axis)
         for i in range(4):
             for j in range(4):
-                add = neighbours(self.f, i, j) + self.f[0, i % 2, j] * SQ[i]
+                add = neighbours(self.f, i, j) + weigh(self.f[0, i % 2, j], i)
                 self.x[i, j] += change[i, j] * KEEP + self.g[i, j] * add
 
 
@@ -446,29 +469,33 @@
         self.coefficient = coefficient
 
     def faces(self):
-        wide_x, wide_y, wide_z, _ = level_scales(self.level)
         count = self.count
-        coefficient = self.coefficient[...][None]
-        ends = iota((4, count, 8, 128), 3) % 64
-        for line in range(4):
-            low, high = face_pair(self.x, 0, line)
-            before, after = (roll(high[:, count - 1 :], 1, 2), roll(low[:, :1], 7, 2))
-            if count > 1:
-                before = jnp.concatenate([before, high[:, : count - 1]], axis=1)
-                after = jnp.concatenate([low[:, 1:], after], axis=1)
-            factor = coefficient * (TAU * wide_x)
-            self.f[0, 0, line] = factor * (before + after)
-            self.f[0, 1, line] = factor * (before - after)
-            low, high = face_pair(self.x, 1, line)
-            factor = coefficient * (TAU * wide_y)
-            self.f[1, 0, line] = factor * roll(high + low, 64, 3)
-            self.f[1, 1, line] = factor * roll(high - low, 64, 3)
-            low, high = face_pair(self.x, 2, line)
-            factor = coefficient * (TAU * wide_z)
-            before = jnp.where(ends < 4, roll(high, 69, 3), roll(high, 4, 3))
-            after = jnp.where(ends >= 60, roll(low, 59, 3), roll(low, 124, 3))
-            self.f[2, 0, line] = factor * (before + after)
-            self.f[2, 1, line] = factor * (before - after)
+        ends = iota((count, 8, 128), 2) % 64
+        value = self.coefficient[...]
+        factors = [
+            (value * (TAU * wide * SQ[0]), value * (TAU * wide * SQ[1]))
+            for wide in level_scales(self.level)[:3]
+        ]
+        for first in range(4):
+            for second in range(4):
+                low, high = face_pair2(self.x, 0, first, second)
+                before, after = (roll(high[count - 1 :], 1, 1), roll(low[:1], 7, 1))
+                if count > 1:
+                    before = jnp.concatenate([before, high[: count - 1]], axis=0)
+                    after = jnp.concatenate([low[1:], after], axis=0)
+                even, odd = factors[0]
+                self.f[0, 0, first, second] = even * (before + after)
+                self.f[0, 1, first, second] = odd * (before - after)
+                low, high = face_pair2(self.x, 1, first, second)
+                even, odd = factors[1]
+                self.f[1, 0, first, second] = even * roll(high + low, 64, 2)
+                self.f[1, 1, first, second] = odd * roll(high - low, 64, 2)
+                low, high = face_pair2(self.x, 2, first, second)
+                even, odd = factors[2]
+                before = jnp.where(ends < 4, roll(high, 69, 2), roll(high, 4, 2))
+                after = jnp.where(ends >= 60, roll(low, 59, 2), roll(low, 124, 2))
+                self.f[2, 0, first, second] = even * (before + after)
+                self.f[2, 1, first, second] = odd * (before - after)
 
     def tables(self):
         inverse_tables(self.g, self.d, self.coefficient[...], self.level)
@@ -505,40 +532,48 @@
         self.e, self.g, self.f, self.h, self.coefficient = (e, g, f, h, coefficient)
 
     def smooth(self, count, beyond):
-        factor = (TAU * level_scales(1)[0]) * self.coefficient[:count][None]
-        low_rows = iota((4, 8, 128), 1) < 4
-        row, lane = (iota((4, count, 8, 128), 2) % 4, iota((4, count, 8, 128), 3))
-        for line in range(4):
-            low, high = face_pair(self.e, 0, line)
-            ha, hb, hc = (high[:, block] for block in range(3))
-            la, lb, lc = (low[:, block] for block in range(3))
-            far = self.h[line] if beyond else hc
-            ta, sa = (roll(ha, 4, 1), roll(la, 4, 1))
-            before = [jnp.where(low_rows, roll(hb, 4, 1), ta), jnp.where(low_rows, ta, hc), jnp.where(low_rows, hb, far)]
-            after = [jnp.where(low_rows, sa, roll(lb, 4, 1)), jnp.where(low_rows, lc, sa), jnp.where(low_rows, far, lb)]
-            before, after = (jnp.stack(before[:count], axis=1), jnp.stack(after[:count], axis=1))
-            self.f[0, 0, line, :, :count] = factor * (before + after)
-            self.f[0, 1, line, :, :count] = factor * (before - after)
-            low, high = face_pair(self.e, 1, line)
-            low, high = (low[:, :count], high[:, :count])
-            before = jnp.where(row == 0, roll(high, 5, 2), roll(high, 1, 2))
-            after = jnp.where(row == 3, roll(low, 3, 2), roll(low, 7, 2))
-            self.f[1, 0, line, :, :count] = factor * (before + after)
-            self.f[1, 1, line, :, :count] = factor * (before - after)
-            low, high = face_pair(self.e, 2, line)
-            low, high = (low[:, :count], high[:, :count])
-            before = jnp.where(lane == 0, roll(high, 1, 3), jnp.where(lane == 1, roll(high, 3, 3), roll(high, 2, 3)))
-            after = jnp.where(
-                lane == 126, roll(low, 125, 3), jnp.where(lane == 127, roll(low, 127, 3), roll(low, 126, 3))
-            )
-            self.f[2, 0, line, :, :count] = factor * (before + after)
-            self.f[2, 1, line, :, :count] = factor * (before - after)
+        value = self.coefficient[:count] * (TAU * level_scales(1)[0])
+        even, odd = (value * SQ[0], value * SQ[1])
+        low_rows = iota((8, 128), 0) < 4
+        row, lane = (iota((count, 8, 128), 1) % 4, iota((count, 8, 128), 2))
+        for first in range(4):
+            for second in range(4):
+                low, high = face_pair2(self.e, 0, first, second)
+                ha, hb, hc = (high[block] for block in range(3))
+                la, lb, lc = (low[block] for block in range(3))
+                far = self.h[first, second] if beyond else hc
+                ta, sa = (roll(ha, 4, 0), roll(la, 4, 0))
+                before = [
+                    jnp.where(low_rows, roll(hb, 4, 0), ta), jnp.where(low_rows, ta, hc), jnp.where(low_rows, hb, far)
+                ]
+                after = [
+                    jnp.where(low_rows, sa, roll(lb, 4, 0)), jnp.where(low_rows, lc, sa), jnp.where(low_rows, far, lb)
+                ]
+                before, after = (jnp.stack(before[:count], axis=0), jnp.stack(after[:count], axis=0))
+                self.f[0, 0, first, second, :count] = even * (before + after)
+                self.f[0, 1, first, second, :count] = odd * (before - after)
+                low, high = face_pair2(self.e, 1, first, second)
+                low, high = (low[:count], high[:count])
+                before = jnp.where(row == 0, roll(high, 5, 1), roll(high, 1, 1))
+                after = jnp.where(row == 3, roll(low, 3, 1), roll(low, 7, 1))
+                self.f[1, 0, first, second, :count] = even * (before + after)
+                self.f[1, 1, first, second, :count] = odd * (before - after)
+                low, high = face_pair2(self.e, 2, first, second)
+                low, high = (low[:count], high[:count])
+                before = jnp.where(
+                    lane == 0, roll(high, 1, 2), jnp.where(lane == 1, roll(high, 3, 2), roll(high, 2, 2))
+                )
+                after = jnp.where(
+                    lane == 126, roll(low, 125, 2), jnp.where(lane == 127, roll(low, 127, 2), roll(low, 126, 2))
+                )
+                self.f[2, 0, first, second, :count] = even * (before + after)
+                self.f[2, 1, first, second, :count] = odd * (before - after)
         for i in range(4):
             for j in range(4):
-                along_z = [self.f[2, k % 2, i, j, :count] * SQ[k] for k in range(4)]
-                add = jnp.stack(along_z, axis=0) + self.f[1, j % 2, i, :, :count] * SQ[j]
-                add = add + self.f[0, i % 2, j, :, :count] * SQ[i]
-                self.e[i, j, :, :count] = self.e[i, j, :, :count] * KEEP + self.g[i, j, :, :count] * add
+                for k in range(4):
+                    add = weigh(self.f[0, i % 2, j, k, :count], i) + weigh(self.f[1, j % 2, i, k, :count], j)
+                    add = add + weigh(self.f[2, k % 2, i, j, :count], k)
+                    self.e[i, j, k, :count] = self.e[i, j, k, :count] * KEEP + self.g[i, j, k, :count] * add
 
 
 def kernel(
@@ -553,7 +588,7 @@
     x3, b3, g3, d3, r3, f3, c3,
     x4, b4, g4, d4, r4, f4, c4,
     px, qx, py0, qy0, pz0, qz0, py1, qy1, pz1, qz1,
-    cs, call, cown, cin,
+    cs, call, cline, cplane, cown, cin,
     ms, mall, my, mz,
     face_send, face_recv,
     c_send, c_recv, c_send2, c_recv2,
@@ -574,7 +609,8 @@
     slow, fast = (gx // 4, lax.rem(gx, 4))
     slow_at = pl.multiple_of(slow * 16, 16)
     slow_at8 = pl.multiple_of(slow * 8, 8)
-    offsets = [(a, b) for a in range(8) for b in range(4) if (a, b) != (0, 0)]
+    nearest = (0, 1, 7, 2, 6, 3, 5, 4)
+    offsets = [(a, b) for a in nearest for b in range(4) if (a, b) != (0, 0)]
 
     def along_x(a, b):
         return {"gx": lax.rem(slow + a, 8) * 4 + lax.rem(fast + b, 4)}
@@ -662,6 +698,16 @@
     fine = Halo(16, 1, x0, b0, g0, d0, r0, t0, f0, coefficient, 1.0, orientation, signs)
     mid = Halo(8, 2, x1, b1, g1, d1, r1, t1, f1, c1, 2.0, None, None)
     links = []
+
+    c_line = [copy(cs, call.at[fast], c_send.at[0, b], c_recv.at[0, b], along_x(0, b)) for b in range(1, 4)]
+    c_copies = [
+        copy(cline, cplane.at[pl.ds(slow_at8, 8)], c_send.at[a, 0], c_recv.at[a, 0], along_x(a, 0))
+        for a in nearest[1:]
+    ]
+
+    def send_line():
+        for item in c_line:
+            item.start()
 
     near_copies = [copy(c1, near_y, near_send.at[0], near_recv.at[0], {"gy": 1 - gy})]
     near_copies[0].start()
@@ -702,7 +748,7 @@
     fine.receive(links[-1], False, lambda: (heard(0), near_step(0)))
     links.append(link(0, 1))
     fine.send(links[-1])
-    fine.receive(links[-1], True, lambda: (heard(1), near_step(1)))
+    fine.receive(links[-1], True, lambda: (heard(1), near_step(1), send_line()))
     row4 = iota((4, 8, 128), 1)
     lane4 = iota((4, 8, 128), 2)
     for j in range(4):
@@ -728,16 +774,17 @@
     mid.receive(links[-1], False, lambda: (heard(2), near_step(2)))
     links.append(link(1, 1))
     mid.send(links[-1])
-    c_copies = [
-        copy(cs, call.at[fast, pl.ds(slow_at8, 8)], c_send.at[a, b], c_recv.at[a, b], along_x(a, b))
-        for a, b in offsets
-    ]
-
     def send_coefficients():
         heard(3)
+        for item in c_line:
+            item.wait_recv()
+        call[fast] = cs[...]
+        lines = [jnp.broadcast_to(call[block, pl.ds(0, 1), :], (8, 128)) for block in range(4)]
+        cline[...] = jnp.where(row8 < 2, jnp.where(row8 == 0, lines[0], lines[1]),
+                               jnp.where(row8 == 2, lines[2], lines[3]))
         for item in c_copies:
             item.start()
-        call[fast, pl.ds(slow_at8, 8), :] = cs[...]
+        cplane[pl.ds(slow_at8, 8), :] = cline[...]
 
     mid.receive(links[-1], True, send_coefficients)
     for j in range(4):
@@ -770,7 +817,7 @@
     for item in c_copies:
         item.wait_recv()
     for block in range(4):
-        cown[block] = call[block, pl.ds(0, 8, stride=8), :]
+        cown[block] = cplane[pl.ds(block, 8, stride=8), :]
     c_around = [
         copy(cown, cin.at[spot], c_send2.at[spot], c_recv2.at[spot], device)
         for spot, device in enumerate(around)
@@ -783,7 +830,7 @@
     links.append(link(1, 2))
     mid.send(links[-1])
     passed = []
-    for a in range(8):
+    for a in nearest:
         for b in range(4):
             if (a, b) != (0, 0):
                 m_copies[a, b].wait_recv()
@@ -999,7 +1046,7 @@
 
     for item in links:
         item.close()
-    for item in near_copies + c_copies + c_around + list(m_copies.values()) + passed:
+    for item in near_copies + c_line + c_copies + c_around + list(m_copies.values()) + passed:
         item.wait_send()
 
 
@@ -1025,7 +1072,7 @@
         mem(4, 2, 4, 4, 8, 128), mem(4, 2, 4, 4, 8, 128), mem(4, 2, 8, 128), mem(4, 2, 8, 128),
     ]
     gathered = [
-        mem(8, 128), mem(4, 64, 128), mem(4, 8, 128), mem(5, 4, 8, 128),
+        mem(8, 128), mem(4, 8, 128), mem(8, 128), mem(64, 128), mem(4, 8, 128), mem(5, 4, 8, 128),
         mem(16, 128), mem(4, 128, 128), mem(4, 128, 128), mem(4, 4, 64, 128),
     ]
     sems = [dma((8, 5)), dma((8, 5)), dma((8, 4)), dma((8, 4)), dma((5,)), dma((5,)),
@@ -1048,7 +1095,7 @@
         out_specs=vmem,
         scratch_shapes=scratch(),
         compiler_params=pltpu.CompilerParams(
-            collective_id=0, has_side_effects=True, vmem_limit_bytes=44 * 1024 * 1024
+            collective_id=0, has_side_effects=True, vmem_limit_bytes=64 * 1024 * 1024 - 65536
         ),
     )(
         source.reshape(4, 4, 4, 16, 128),

time: 66.4 us -> 63.2 us (0.952)
  Pallas kernels: 62.9 us -> 61.2 us
  local copies, waits for them, and re-layouts: 3.33 us -> 1.88 us
    pallas_call x1, Pallas kernels: 62.9 us -> 61.2 us  [local(): pl.pallas_call(kernel, out_shape=jax.ShapeDtypeStruct((4, 4, 4, 16, 128),...]
    unnamed x7 -> x1, local copies, waits for them, and re-layouts: 3.33 us -> 1.88 us
where the time goes in v2:
time: 63.2 us; the launch traced here: 63.1 us
  Pallas kernels  61.2 us (97%)
  local copies, waits for them, and re-layouts  1.88 us (3%)
    pallas_call x1, Pallas kernels, local(): pl.pallas_call(kernel, out_shape=jax.ShapeDtypeStruct((4, 4, 4, 16, 128),...  61.2 us
    unnamed x1, local copies, waits for them, and re-layouts  1.88 us

profile of v2, /device:TPU:1, one launch (start us, length us, event | category | flops | bytes accessed | tf_op | source)
XLA Modules:
  0.0 63.1 jit_solution(17252044387022208064)
XLA Ops:
  0.0 61.2 %shard_map.37 = f32[4,4,4,16,128]{4,3,2,1,0:T(8,128)} custom-call(f32[4,4,4,16,128]{4,3,2,1,0:T(8,128)} %bitcast.5, f32[16,128]{1,0:T(8,128)} %bitcast.7, s32[6,16,128]{2,1,0:T(8,128)} %bitcast.6), custom_call_target="tpu_custom_call" | custom-call | tf_op jit(solution)/shard_map/pallas_call | solution.py:1091
  61.2 1.9 %copy.5 = f32[4,4,4,4,4,128]{5,4,3,2,1,0:T(4,128)} copy(f32[4,4,4,4,4,128]{5,4,3,2,1,0:T(4,128)} %bitcast.4) | data formatting | bytes 1048576

commit v3 on v2

--- a/solution.py
+++ b/solution.py
@@ -264,7 +264,7 @@
         self.coefficient, self.wide = (coefficient, wide)
         self.orientation, self.signs = (orientation, signs)
 
-    def send(self, link):
+    def send(self, link, after_x=None):
         rows, stride = (self.rows, self.stride)
         low_rows = iota((4, 8, 128), 1) < 4
         lane = iota((rows, 128), 1)
@@ -280,6 +280,8 @@
             link.px[0, j] = jnp.where(low_rows, firsts[j][0], lasts[j + 2][0])
             link.px[1, j] = jnp.where(low_rows, firsts[j][1], lasts[j + 2][1])
         link.start_x()
+        if after_x is not None:
+            after_x()
         packed_high = packed_low = jnp.zeros((rows, 128), F32)
         for i in range(4):
             low, high = face_pair(self.x, 2, i)
@@ -581,7 +583,7 @@
     coefficient_in,
     orientation_in,
     out,
-    source, coefficient, orientation, input_sem,
+    source, coefficient, orientation, input_sem, output_sem,
     x0, b0, g0, d0, r0, t0, f0, signs,
     x1, b1, g1, d1, r1, t1, f1, c1, w1, v1,
     x2, b2, g2, d2, r2, f2, c2,
@@ -680,8 +682,6 @@
         if step < 3:
             tell(step + 1)
 
-    tell(0)
-
     def link(level, step):
         spot = 4 * level + step
         py, qy, pz, qz = (py0, qy0, pz0, qz0) if level == 0 else (py1, qy1, pz1, qz1)
@@ -710,7 +710,6 @@
             item.start()
 
     near_copies = [copy(c1, near_y, near_send.at[0], near_recv.at[0], {"gy": 1 - gy})]
-    near_copies[0].start()
     ring = iota((8, 128), 0) % 4
 
     def near_step(step):
@@ -744,11 +743,13 @@
             inverse_tables(ge, de, ce[...], 1)
 
     links.append(link(0, 0))
-    fine.send(links[-1])
-    fine.receive(links[-1], False, lambda: (heard(0), near_step(0)))
+    fine.send(links[-1], lambda: tell(0))
+    near_copies[0].start()
+    fine.receive(links[-1], False, lambda: near_step(0))
+    heard(0)
     links.append(link(0, 1))
     fine.send(links[-1])
-    fine.receive(links[-1], True, lambda: (heard(1), near_step(1), send_line()))
+    fine.receive(links[-1], True, lambda: near_step(1))
     row4 = iota((4, 8, 128), 1)
     lane4 = iota((4, 8, 128), 2)
     for j in range(4):
@@ -770,7 +771,7 @@
 
     first_guess(x1, b1, g1)
     links.append(link(1, 0))
-    mid.send(links[-1])
+    mid.send(links[-1], lambda: (heard(1), send_line()))
     mid.receive(links[-1], False, lambda: (heard(2), near_step(2)))
     links.append(link(1, 1))
     mid.send(links[-1])
@@ -1034,18 +1035,21 @@
     fine.send(links[-1])
     fine.receive(links[-1], False)
 
+    for j in range(4):
+        for i, value in enumerate(from_modes(*[x0[i, j] for i in range(4)])):
+            x0[i, j] = value
+    outputs = []
     for i in range(4):
         for k, value in enumerate(from_modes(*[x0[i, :, k] for k in range(4)])):
-            out[i, :, k] = value
-    for i in range(4):
-        for j, value in enumerate(from_modes(*[out[i, j] for j in range(4)])):
-            out[i, j] = value
-    for j in range(4):
-        for i, value in enumerate(from_modes(*[out[i, j] for i in range(4)])):
-            out[i, j] = value
-
+            x0[i, :, k] = value
+        for j, value in enumerate(from_modes(*[x0[i, j] for j in range(4)])):
+            x0[i, j] = value
+        outputs.append(pltpu.make_async_copy(x0.at[i], out.at[i], output_sem.at[i]))
+        outputs[-1].start()
     for item in links:
         item.close()
+    for item in outputs:
+        item.wait()
     for item in near_copies + c_line + c_copies + c_around + list(m_copies.values()) + passed:
         item.wait_send()
 
@@ -1056,7 +1060,7 @@
 
     modes = (4, 4, 4)
     dma = pltpu.SemaphoreType.DMA
-    inputs = [mem(*modes, 16, 128), mem(16, 128), pltpu.VMEM((6, 16, 128), jnp.int32), dma((3,))]
+    inputs = [mem(*modes, 16, 128), mem(16, 128), pltpu.VMEM((6, 16, 128), jnp.int32), dma((3,)), dma((4,))]
     level0 = [mem(*modes, 16, 128)] * 5 + [
         mem(3, 2, 4, 4, 16, 128), mem(3, 2, 4, 4, 16, 128), mem(6, 2, 4, 16, 128)
     ]
@@ -1087,12 +1091,11 @@
 
 
 def local(source, coefficient, orientation):
-    vmem = pl.BlockSpec(memory_space=pltpu.VMEM)
     out = pl.pallas_call(
         kernel,
         out_shape=jax.ShapeDtypeStruct((4, 4, 4, 16, 128), F32),
         in_specs=[pl.BlockSpec(memory_space=pl.ANY)] * 3,
-        out_specs=vmem,
+        out_specs=pl.BlockSpec(memory_space=pl.ANY),
         scratch_shapes=scratch(),
         compiler_params=pltpu.CompilerParams(
             collective_id=0, has_side_effects=True, vmem_limit_bytes=64 * 1024 * 1024 - 65536

time: 63.2 us -> 63.2 us (level)
  no operation moved by 1% of the time
where the time goes in v3:
time: 63.2 us; the launch traced here: 63 us
  Pallas kernels  61.1 us (97%)
  local copies, waits for them, and re-layouts  1.88 us (3%)
    pallas_call x1, Pallas kernels, local(): pl.pallas_call(kernel, out_shape=jax.ShapeDtypeStruct((4, 4, 4, 16, 128),...  61.1 us
    unnamed x1, local copies, waits for them, and re-layouts  1.88 us

profile of v3, /device:TPU:1, one launch (start us, length us, event | category | flops | bytes accessed | tf_op | source)
XLA Modules:
  0.0 63.0 jit_solution(9370084178718666923)
XLA Ops:
  0.0 61.1 %shard_map.37 = f32[4,4,4,16,128]{4,3,2,1,0:T(8,128)} custom-call(f32[4,4,4,16,128]{4,3,2,1,0:T(8,128)} %bitcast.5, f32[16,128]{1,0:T(8,128)} %bitcast.7, s32[6,16,128]{2,1,0:T(8,128)} %bitcast.6), custom_call_target="tpu_custom_call" | custom-call | tf_op jit(solution)/shard_map/pallas_call | solution.py:1094
  61.1 1.9 %copy.5 = f32[4,4,4,4,4,128]{5,4,3,2,1,0:T(4,128)} copy(f32[4,4,4,4,4,128]{5,4,3,2,1,0:T(4,128)} %bitcast.4) | data formatting | bytes 1048576
